TPU v7x, 256 devices: a whole 4x4x8 slice. The times are simulated.
256 devices in a mesh: tm: 16 (over x_lo, z), sx: 2 (over x_hi), sy: 8 (over y, core).
Axes of the slice: x: 4 (x_hi: 2, x_lo: 2; x = x_hi * 2 + x_lo), y: 4, z: 8, core: 2. Of those that a mesh axis runs over, the one named last changes fastest.
Arguments:
- initial: float32 [2, 512, 4096], P(None, 'sx', 'sy'), may hold values from -1 to 1
- forcing: float32 [2, 512, 4096], P(None, 'sx', 'sy'), may hold values from -3 to 3
- start_guess: float32 [16, 2, 512, 4096], P('tm', None, 'sx', 'sy'), may hold values from -1 to 1
Outputs:
- solution: float32 [32, 2, 512, 4096], P('tm', None, 'sx', 'sy')
All inputs are finite; a program needn't handle non-finite values.
Results may differ from a plain program's by a relative error of at most 0.003.
Values sent between devices are 32-bit elements; how exact they have to be, the bound alone decides.
A program may use at most 64 MiB of HBM per device.

v0:
```python
import jax
import jax.numpy as jnp
from jax import lax
from jax.sharding import PartitionSpec as P

VISCOSITY = 0.5
COURANT = 0.7


def padded_2(shard, sides, width):
    for axis, dim in sides:
        devices, length = (lax.axis_size(axis), shard.shape[dim])
        up = [(i, (i + 1) % devices) for i in range(devices)]
        down = [(j, i) for i, j in up]
        last = lax.slice_in_dim(shard, length - width, length, axis=dim)
        leading = lax.slice_in_dim(shard, 0, width, axis=dim)
        before = lax.ppermute(last, axis, up)
        after = lax.ppermute(leading, axis, down)
        shard = jnp.concatenate([before, shard, after], axis=dim)
    return shard


def shifted(block, axis, distance):
    devices = range(lax.axis_size(axis))
    route = [(i - distance, i) for i in devices if i - distance in devices]
    return lax.ppermute(block, axis, route)


def advance(padded, forcing, step_size):
    centre = padded[..., 1:-1, 1:-1]
    west_cell = padded[..., :-2, 1:-1]
    east_cell = padded[..., 2:, 1:-1]
    south_cell = padded[..., 1:-1, :-2]
    north_cell = padded[..., 1:-1, 2:]
    first_speed = centre[..., 0:1, :, :]
    second_speed = centre[..., 1:2, :, :]
    spread = east_cell + west_cell + north_cell + south_cell - 4.0 * centre
    carried = (
        jnp.maximum(first_speed, 0.0) * (centre - west_cell)
        + jnp.minimum(first_speed, 0.0) * (east_cell - centre)
        + jnp.maximum(second_speed, 0.0) * (centre - south_cell)
        + jnp.minimum(second_speed, 0.0) * (north_cell - centre)
    )
    return centre + step_size * (VISCOSITY * spread - carried + forcing)


def add_rim(state):
    return padded_2(state, (("sx", 1), ("sy", 2)), 1)


def earlier(state, initial, position, stride):
    arrived = shifted(state, "tm", stride)
    return jnp.where(position < stride, initial, arrived)


def descend(
    values, level_rhs, prior, image_prior, stride, initial, forcing, position, chain_size, fine_step
):
    step_size = 2 * stride * fine_step
    if 2 * stride == chain_size:
        first_point = image_prior + level_rhs
        prior_second = earlier(first_point, initial, position, stride)
        second = advance(add_rim(prior_second), forcing, step_size) + level_rhs
        return jnp.where(
            position == stride - 1,
            first_point,
            jnp.where(position == chain_size - 1, second, values),
        )
    relax_here = position % (2 * stride) == stride - 1
    coarse_here = position % (2 * stride) == 2 * stride - 1
    relaxed = jnp.where(relax_here, image_prior + level_rhs, values)
    before, coarse_prior = shifted((relaxed, prior), "tm", stride)
    coarse_rim = add_rim(coarse_prior)
    before_rim = add_rim(before)
    coarse_image = advance(coarse_rim, forcing, 2 * step_size)
    residual = level_rhs - (relaxed - advance(before_rim, forcing, step_size))
    coarse_rhs = residual + relaxed - coarse_image
    coarse = descend(
        relaxed,
        coarse_rhs,
        coarse_prior,
        coarse_image,
        2 * stride,
        initial,
        forcing,
        position,
        chain_size,
        fine_step,
    )
    updated = jnp.where(coarse_here, coarse, relaxed)
    prior_again = earlier(updated, initial, position, stride)
    final_state = advance(add_rim(prior_again), forcing, step_size) + level_rhs
    return jnp.where(relax_here, final_state, updated)


def body(initial, forcing, start_guess):
    position = lax.axis_index("tm")
    chain_size = lax.axis_size("tm")
    fine_step = COURANT / (chain_size * (2.0 + 4.0 * VISCOSITY))
    own_point = start_guess[0]
    prior = earlier(own_point, initial, position, 1)
    padded = add_rim(prior)
    middle = advance(padded, forcing, fine_step)
    image_prior = advance(padded, forcing, 2 * fine_step)
    ahead_state = advance(add_rim(middle), forcing, fine_step)
    residual = 0.0 - (own_point - ahead_state)
    coarse_rhs = residual + own_point - image_prior
    coarse = descend(
        own_point,
        coarse_rhs,
        prior,
        image_prior,
        1,
        initial,
        forcing,
        position,
        chain_size,
        fine_step,
    )
    prior_again = earlier(coarse, initial, position, 1)
    final_state = advance(add_rim(prior_again), forcing, fine_step)
    return jnp.stack((final_state, coarse))


def solution(mesh):
    in_specs = (P(None, "sx", "sy"), P(None, "sx", "sy"), P("tm", None, "sx", "sy"))
    out_specs = P("tm", None, "sx", "sy")
    return jax.shard_map(body, mesh=mesh, in_specs=in_specs, out_specs=out_specs, check_vma=False)
```

profile of v0, /device:TPU:2, one launch (start us, length us, event | category | flops | bytes accessed | tf_op | source)
XLA Modules:
  0.0 567.0 jit_solution(2435578746979790487)
XLA Ops:
  0.0 3.8 collective-permute-start
  3.8 27.3 %collective-permute-done = f32[2,256,512]{2,1,0:T(8,128)S(1)} collective-permute-done((f32[2,256,512]{2,1,0:T(8,128)}, f32[2,256,512]{2,1,0:T(8,128)S(1)}, u32[]{:S(2)}, u32[]{:S(2)}) %collective-permute-start) | collective-permute-done | bytes 1048608 | tf_op jit(solution)/shard_map/ppermute | solution.py:26
  31.3 2.6 collective-permute-start.8
  36.5 2.5 collective-permute-done.9
  40.0 3.6 collective-permute-done.10
  43.6 3.1 collective-permute-done.11
  46.7 2.8 multiply_add_fusion.1
  50.7 2.4 collective-permute-start.13
  53.2 2.0 collective-permute-start.1
  56.8 3.2 collective-permute-done.14
  60.0 3.1 collective-permute-done.15
  63.1 3.3 add_select_fusion.2
  68.4 15.2 %collective-permute-done.1 = f32[2,256,512]{2,1,0:T(8,128)} collective-permute-done((f32[2,256,512]{2,1,0:T(8,128)S(1)}, f32[2,256,512]{2,1,0:T(8,128)}, u32[]{:S(2)}, u32[]{:S(2)}) %collective-permute-start.1) | collective-permute-done | bytes 1048608 | tf_op jit(solution)/shard_map/ppermute | solution.py:26
  85.5 2.4 collective-permute-start.22
  91.3 37.0 %collective-permute-done.16 = f32[2,256,512]{2,1,0:T(8,128)S(1)} collective-permute-done((f32[2,256,512]{2,1,0:T(8,128)}, f32[2,256,512]{2,1,0:T(8,128)S(1)}, u32[]{:S(2)}, u32[]{:S(2)}) %collective-permute-start.16) | collective-permute-done | bytes 1048608 | tf_op jit(solution)/shard_map/ppermute | solution.py:26
  129.6 2.4 collective-permute-start.18
  137.2 3.1 collective-permute-done.24
  140.3 3.1 collective-permute-done.20
  143.5 7.5 %add_select_fusion.1 = (f32[2,256,512]{2,1,0:T(8,128)}, f32[2,256,512]{2,1,0:T(8,128)}) fusion(f32[2,256,512]{2,1,0:T(8,128)} %get-tuple-element.11, pred[]{:T(512)S(6)} %eq.33, f32[2,256,512]{2,1,0:T(8,128)S(1)} %copy-done.2, f32[2,256,512]{2,1,0:T(8,128)S(1)} %collective-permute-done.16, f32[2,256,512]{2,1,0:T(8,128)S(1)} %copy-done, ...), kind=kLoop, calls=%fused_computation.341 | loop fusion | flops 16777216 | bytes 11558977 | tf_op jit(solution)/shard_map/jit(_where)/select_n | solution.py:71
  154.1 2.6 collective-permute-start.31
  156.7 3.8 collective-permute-start.3
  160.7 37.0 %collective-permute-done.25 = f32[2,256,512]{2,1,0:T(8,128)S(1)} collective-permute-done((f32[2,256,512]{2,1,0:T(8,128)}, f32[2,256,512]{2,1,0:T(8,128)S(1)}, u32[]{:S(2)}, u32[]{:S(2)}) %collective-permute-start.25) | collective-permute-done | bytes 1048608 | tf_op jit(solution)/shard_map/ppermute | solution.py:26
  197.8 23.7 %collective-permute-start.26 = (f32[2,1,512]{2,1,0:T(1,128)S(1)}, f32[2,1,512]{2,1,0:T(1,128)S(1)}, u32[]{:S(2)}, u32[]{:S(2)}) collective-permute-start(f32[2,1,512]{2,1,0:T(1,128)S(1)} %get-tuple-element.84), channel_id=1, source_target_pairs={{8,0},{0,8},{9,1},{1,9},{10,2},{2,10},{11,3},{3,11},{12,4},{4,12},... | collective-permute-start | bytes 12296 | tf_op jit(solution)/shard_map/ppermute | solution.py:18
  223.1 3.5 collective-permute-done.27
  230.7 3.7 collective-permute-done.29
  234.4 5.4 add_select_fusion
  239.8 6.9 %collective-permute-start.34 = (f32[2,256,512]{2,1,0:T(8,128)S(1)}, f32[2,256,512]{2,1,0:T(8,128)S(1)}, u32[]{:S(2)}, u32[]{:S(2)}) collective-permute-start(f32[2,256,512]{2,1,0:T(8,128)S(1)} %get-tuple-element.7), channel_id=1, source_target_pairs={{0,64},{16,80},{32,96},{48,112},{64,128},{80,144},{96,160},{112,17... | collective-permute-start | bytes 3145736 | tf_op jit(solution)/shard_map/ppermute | solution.py:26
  246.7 2.0 collective-permute-start.4
  250.7 19.6 %collective-permute-done.34 = f32[2,256,512]{2,1,0:T(8,128)S(1)} collective-permute-done((f32[2,256,512]{2,1,0:T(8,128)S(1)}, f32[2,256,512]{2,1,0:T(8,128)S(1)}, u32[]{:S(2)}, u32[]{:S(2)}) %collective-permute-start.34) | collective-permute-done | bytes 1048608 | tf_op jit(solution)/shard_map/ppermute | solution.py:26
  271.7 2.2 collective-permute-start.36
  278.1 3.1 collective-permute-done.7
  281.2 3.1 collective-permute-done.38
  284.3 5.5 fusion.235
  291.1 24.3 %collective-permute-done.39 = f32[2,256,512]{2,1,0:T(8,128)} collective-permute-done((f32[2,256,512]{2,1,0:T(8,128)S(1)}, f32[2,256,512]{2,1,0:T(8,128)}, u32[]{:S(2)}, u32[]{:S(2)}) %collective-permute-start.39) | collective-permute-done | bytes 1048608 | tf_op jit(solution)/shard_map/ppermute | solution.py:26
  316.8 2.3 collective-permute-start.40
  322.0 2.4 collective-permute-done.41
  325.4 3.2 collective-permute-done.42
  328.6 3.1 collective-permute-done.43
  331.8 3.2 fusion.86
  335.0 5.7 %collective-permute-start.44 = (f32[2,256,512]{2,1,0:T(8,128)}, f32[2,256,512]{2,1,0:T(8,128)}, u32[]{:S(2)}, u32[]{:S(2)}) collective-permute-start(f32[2,256,512]{2,1,0:T(8,128)} %fusion.86), channel_id=1, source_target_pairs={{0,64},{16,80},{32,96},{48,112},{64,128},{80,144},{96,160},{112,17... | collective-permute-start | bytes 3145736 | tf_op jit(solution)/shard_map/ppermute | solution.py:26
  340.7 47.7 %collective-permute-done.44 = f32[2,256,512]{2,1,0:T(8,128)} collective-permute-done((f32[2,256,512]{2,1,0:T(8,128)}, f32[2,256,512]{2,1,0:T(8,128)}, u32[]{:S(2)}, u32[]{:S(2)}) %collective-permute-start.44) | collective-permute-done | bytes 1048608 | tf_op jit(solution)/shard_map/ppermute | solution.py:26
  391.3 2.2 collective-permute-start.46
  397.4 3.2 collective-permute-done.47
  400.6 3.1 collective-permute-done.48
  403.7 4.3 fusion.66
  408.0 4.2 collective-permute-start.49
  412.2 46.8 %collective-permute-done.49 = f32[2,256,512]{2,1,0:T(8,128)} collective-permute-done((f32[2,256,512]{2,1,0:T(8,128)}, f32[2,256,512]{2,1,0:T(8,128)}, u32[]{:S(2)}, u32[]{:S(2)}) %collective-permute-start.49) | collective-permute-done | bytes 1048608 | tf_op jit(solution)/shard_map/ppermute | solution.py:26
  461.3 2.8 collective-permute-start.51
  467.3 3.5 collective-permute-done.52
  470.8 3.1 collective-permute-done.53
  474.0 3.5 fusion.47
  477.5 1.9 collective-permute-start.54
  479.4 24.8 %collective-permute-done.54 = f32[2,256,512]{2,1,0:T(8,128)S(1)} collective-permute-done((f32[2,256,512]{2,1,0:T(8,128)S(1)}, f32[2,256,512]{2,1,0:T(8,128)S(1)}, u32[]{:S(2)}, u32[]{:S(2)}) %collective-permute-start.54) | collective-permute-done | bytes 1048608 | tf_op jit(solution)/shard_map/ppermute | solution.py:26
  504.5 3.5 collective-permute-start.55
  509.7 3.4 collective-permute-done.56
  514.1 3.2 collective-permute-done.57
  517.3 3.1 collective-permute-done.58
  520.4 2.2 fusion.28
  522.6 1.9 collective-permute-start.59
  524.5 25.7 %collective-permute-done.59 = f32[2,256,512]{2,1,0:T(8,128)S(1)} collective-permute-done((f32[2,256,512]{2,1,0:T(8,128)S(1)}, f32[2,256,512]{2,1,0:T(8,128)S(1)}, u32[]{:S(2)}, u32[]{:S(2)}) %collective-permute-start.59) | collective-permute-done | bytes 1048608 | tf_op jit(solution)/shard_map/ppermute | solution.py:26
  550.7 3.4 collective-permute-start.61
  556.8 3.1 collective-permute-done.62
  559.9 3.1 collective-permute-done.63
  563.1 2.1 fusion.10
  (150 shorter events, 62.9 us)
Async XLA Ops:
  0.0 31.1 %collective-permute-start = (f32[2,256,512]{2,1,0:T(8,128)}, f32[2,256,512]{2,1,0:T(8,128)S(1)}, u32[]{:S(2)}, u32[]{:S(2)}) collective-permute-start(f32[2,256,512]{2,1,0:T(8,128)} %bitcast.112), channel_id=1, source_target_pairs={{0,16},{16,32},{32,48},{48,64},{64,80},{80,96},{96,112},{112,128},... | collective-permute-start | bytes 3145736 | tf_op jit(solution)/shard_map/ppermute | solution.py:26
  31.3 5.2 collective-permute-start.8
  33.9 5.1 collective-permute-start.9
  39.2 4.4 collective-permute-start.10
  39.6 7.1 %collective-permute-start.11 = (f32[2,258,1]{2,1,0:T(8,128)S(1)}, f32[2,258,1]{2,1,0:T(8,128)S(1)}, u32[]{:S(2)}, u32[]{:S(2)}) collective-permute-start(f32[2,258,1]{2,1,0:T(8,128)S(1)} %get-tuple-element.40), channel_id=1, source_target_pairs={{0,1},{1,2},{2,3},{3,4},{4,5},{5,6},{6,7},{7,0},{8,9},{9,10},{10,1... | collective-permute-start | bytes 6200 | tf_op jit(solution)/shard_map/ppermute | solution.py:17
  49.5 5.7 %collective-permute-start.12 = (f32[2,1,512]{2,1,0:T(1,128)S(1)}, f32[2,1,512]{2,1,0:T(1,128)S(1)}, u32[]{:S(2)}, u32[]{:S(2)}) collective-permute-start(f32[2,1,512]{2,1,0:T(1,128)S(1)} %get-tuple-element.108), channel_id=1, source_target_pairs={{8,0},{0,8},{9,1},{1,9},{10,2},{2,10},{11,3},{3,11},{12,4},{4,12},... | collective-permute-start | bytes 12296 | tf_op jit(solution)/shard_map/ppermute | solution.py:18
  50.7 5.1 collective-permute-start.13
  53.2 30.4 %collective-permute-start.1 = (f32[2,256,512]{2,1,0:T(8,128)S(1)}, f32[2,256,512]{2,1,0:T(8,128)}, u32[]{:S(2)}, u32[]{:S(2)}) collective-permute-start(f32[2,256,512]{2,1,0:T(8,128)S(1)} %broadcast_select_fusion.5), channel_id=1, source_target_pairs={{0,16},{16,32},{32,48},{48,64},{64,80},{80,96},{96,112},{112,128},... | collective-permute-start | bytes 3145736 | tf_op jit(solution)/shard_map/ppermute | solution.py:26
  56.0 4.0 collective-permute-start.14
  56.0 7.1 %collective-permute-start.15 = (f32[2,258,1]{2,1,0:T(8,128)S(1)}, f32[2,258,1]{2,1,0:T(8,128)S(1)}, u32[]{:S(2)}, u32[]{:S(2)}) collective-permute-start(f32[2,258,1]{2,1,0:T(8,128)S(1)} %get-tuple-element.38), channel_id=1, source_target_pairs={{0,1},{1,2},{2,3},{3,4},{4,5},{5,6},{6,7},{7,0},{8,9},{9,10},{10,1... | collective-permute-start | bytes 6200 | tf_op jit(solution)/shard_map/ppermute | solution.py:17
  66.5 61.9 %collective-permute-start.16 = (f32[2,256,512]{2,1,0:T(8,128)}, f32[2,256,512]{2,1,0:T(8,128)S(1)}, u32[]{:S(2)}, u32[]{:S(2)}) collective-permute-start(f32[2,256,512]{2,1,0:T(8,128)} %get-tuple-element.11), channel_id=1, source_target_pairs={{0,16},{16,32},{32,48},{48,64},{64,80},{80,96},{96,112},{112,128},... | collective-permute-start | bytes 3145736 | tf_op jit(solution)/shard_map/ppermute | solution.py:26
  84.4 47.6 %collective-permute-start.21 = (f32[2,1,512]{2,1,0:T(1,128)S(1)}, f32[2,1,512]{2,1,0:T(1,128)S(1)}, u32[]{:S(2)}, u32[]{:S(2)}) collective-permute-start(f32[2,1,512]{2,1,0:T(1,128)S(1)} %get-tuple-element.105), channel_id=1, source_target_pairs={{8,0},{0,8},{9,1},{1,9},{10,2},{2,10},{11,3},{3,11},{12,4},{4,12},... | collective-permute-start | bytes 12296 | tf_op jit(solution)/shard_map/ppermute | solution.py:18
  85.5 46.4 %collective-permute-start.22 = (f32[2,1,512]{2,1,0:T(1,128)S(1)}, f32[2,1,512]{2,1,0:T(1,128)S(1)}, u32[]{:S(2)}, u32[]{:S(2)}) collective-permute-start(f32[2,1,512]{2,1,0:T(1,128)S(1)} %get-tuple-element.106), channel_id=1, source_target_pairs={{0,8},{8,0},{1,9},{9,1},{2,10},{10,2},{3,11},{11,3},{4,12},{12,4},... | collective-permute-start | bytes 12296 | tf_op jit(solution)/shard_map/ppermute | solution.py:17
  88.0 64.9 %collective-permute-start.2 = (f32[2,256,512]{2,1,0:T(8,128)}, f32[2,256,512]{2,1,0:T(8,128)S(1)}, u32[]{:S(2)}, u32[]{:S(2)}) collective-permute-start(f32[2,256,512]{2,1,0:T(8,128)} %collective-permute-done.1), channel_id=1, source_target_pairs={{0,32},{16,48},{32,64},{48,80},{64,96},{80,112},{96,128},{112,144}... | collective-permute-start | bytes 3145736 | tf_op jit(solution)/shard_map/ppermute | solution.py:26
  128.4 5.4 collective-permute-start.17
  129.6 5.1 collective-permute-start.18
  133.2 4.0 collective-permute-start.23
  133.2 7.1 %collective-permute-start.24 = (f32[2,258,1]{2,1,0:T(8,128)S(1)}, f32[2,258,1]{2,1,0:T(8,128)S(1)}, u32[]{:S(2)}, u32[]{:S(2)}) collective-permute-start(f32[2,258,1]{2,1,0:T(8,128)S(1)} %get-tuple-element.35), channel_id=1, source_target_pairs={{0,1},{1,2},{2,3},{3,4},{4,5},{5,6},{6,7},{7,0},{8,9},{9,10},{10,1... | collective-permute-start | bytes 6200 | tf_op jit(solution)/shard_map/ppermute | solution.py:17
  134.8 5.5 collective-permute-start.19
  136.4 7.1 %collective-permute-start.20 = (f32[2,258,1]{2,1,0:T(8,128)S(1)}, f32[2,258,1]{2,1,0:T(8,128)S(1)}, u32[]{:S(2)}, u32[]{:S(2)}) collective-permute-start(f32[2,258,1]{2,1,0:T(8,128)S(1)} %get-tuple-element.34), channel_id=1, source_target_pairs={{0,1},{1,2},{2,3},{3,4},{4,5},{5,6},{6,7},{7,0},{8,9},{9,10},{10,1... | collective-permute-start | bytes 6200 | tf_op jit(solution)/shard_map/ppermute | solution.py:17
  151.0 46.8 %collective-permute-start.25 = (f32[2,256,512]{2,1,0:T(8,128)}, f32[2,256,512]{2,1,0:T(8,128)S(1)}, u32[]{:S(2)}, u32[]{:S(2)}) collective-permute-start(f32[2,256,512]{2,1,0:T(8,128)} %get-tuple-element.9), channel_id=1, source_target_pairs={{0,32},{16,48},{32,64},{48,80},{64,96},{80,112},{96,128},{112,144}... | collective-permute-start | bytes 3145736 | tf_op jit(solution)/shard_map/ppermute | solution.py:26
  152.9 68.7 %collective-permute-start.30 = (f32[2,1,512]{2,1,0:T(1,128)S(1)}, f32[2,1,512]{2,1,0:T(1,128)S(1)}, u32[]{:S(2)}, u32[]{:S(2)}) collective-permute-start(f32[2,1,512]{2,1,0:T(1,128)S(1)} %get-tuple-element.93), channel_id=1, source_target_pairs={{8,0},{0,8},{9,1},{1,9},{10,2},{2,10},{11,3},{3,11},{12,4},{4,12},... | collective-permute-start | bytes 12296 | tf_op jit(solution)/shard_map/ppermute | solution.py:18
  154.1 67.5 %collective-permute-start.31 = (f32[2,1,512]{2,1,0:T(1,128)S(1)}, f32[2,1,512]{2,1,0:T(1,128)S(1)}, u32[]{:S(2)}, u32[]{:S(2)}) collective-permute-start(f32[2,1,512]{2,1,0:T(1,128)S(1)} %get-tuple-element.94), channel_id=1, source_target_pairs={{0,8},{8,0},{1,9},{9,1},{2,10},{10,2},{3,11},{11,3},{4,12},{12,4},... | collective-permute-start | bytes 12296 | tf_op jit(solution)/shard_map/ppermute | solution.py:17
  156.7 90.0 %collective-permute-start.3 = (f32[2,256,512]{2,1,0:T(8,128)S(1)}, f32[2,256,512]{2,1,0:T(8,128)S(1)}, u32[]{:S(2)}, u32[]{:S(2)}) collective-permute-start(f32[2,256,512]{2,1,0:T(8,128)S(1)} %collective-permute-done.2), channel_id=1, source_target_pairs={{0,64},{16,80},{32,96},{48,112},{64,128},{80,144},{96,160},{112,17... | collective-permute-start | bytes 3145736 | tf_op jit(solution)/shard_map/ppermute | solution.py:26
  197.8 25.3 %collective-permute-start.26 = (f32[2,1,512]{2,1,0:T(1,128)S(1)}, f32[2,1,512]{2,1,0:T(1,128)S(1)}, u32[]{:S(2)}, u32[]{:S(2)}) collective-permute-start(f32[2,1,512]{2,1,0:T(1,128)S(1)} %get-tuple-element.84), channel_id=1, source_target_pairs={{8,0},{0,8},{9,1},{1,9},{10,2},{2,10},{11,3},{3,11},{12,4},{4,12},... | collective-permute-start | bytes 12296 | tf_op jit(solution)/shard_map/ppermute | solution.py:18
  221.5 5.1 collective-permute-start.27
  221.7 5.8 %collective-permute-start.32 = (f32[2,258,1]{2,1,0:T(8,128)S(1)}, f32[2,258,1]{2,1,0:T(8,128)S(1)}, u32[]{:S(2)}, u32[]{:S(2)}) collective-permute-start(f32[2,258,1]{2,1,0:T(8,128)S(1)} %get-tuple-element.32), channel_id=1, source_target_pairs={{1,0},{2,1},{3,2},{4,3},{5,4},{6,5},{7,6},{0,7},{9,8},{10,9},{11,1... | collective-permute-start | bytes 6200 | tf_op jit(solution)/shard_map/ppermute | solution.py:18
  221.8 7.6 %collective-permute-start.33 = (f32[2,258,1]{2,1,0:T(8,128)S(1)}, f32[2,258,1]{2,1,0:T(8,128)S(1)}, u32[]{:S(2)}, u32[]{:S(2)}) collective-permute-start(f32[2,258,1]{2,1,0:T(8,128)S(1)} %get-tuple-element.31), channel_id=1, source_target_pairs={{0,1},{1,2},{2,3},{3,4},{4,5},{5,6},{6,7},{7,0},{8,9},{9,10},{10,1... | collective-permute-start | bytes 6200 | tf_op jit(solution)/shard_map/ppermute | solution.py:17
  226.7 4.0 collective-permute-start.28
  226.8 7.6 %collective-permute-start.29 = (f32[2,258,1]{2,1,0:T(8,128)S(1)}, f32[2,258,1]{2,1,0:T(8,128)S(1)}, u32[]{:S(2)}, u32[]{:S(2)}) collective-permute-start(f32[2,258,1]{2,1,0:T(8,128)S(1)} %get-tuple-element.30), channel_id=1, source_target_pairs={{0,1},{1,2},{2,3},{3,4},{4,5},{5,6},{6,7},{7,0},{8,9},{9,10},{10,1... | collective-permute-start | bytes 6200 | tf_op jit(solution)/shard_map/ppermute | solution.py:17
  239.8 30.5 %collective-permute-start.34 = (f32[2,256,512]{2,1,0:T(8,128)S(1)}, f32[2,256,512]{2,1,0:T(8,128)S(1)}, u32[]{:S(2)}, u32[]{:S(2)}) collective-permute-start(f32[2,256,512]{2,1,0:T(8,128)S(1)} %get-tuple-element.7), channel_id=1, source_target_pairs={{0,64},{16,80},{32,96},{48,112},{64,128},{80,144},{96,160},{112,17... | collective-permute-start | bytes 3145736 | tf_op jit(solution)/shard_map/ppermute | solution.py:26
  246.7 27.2 %collective-permute-start.4 = (f32[2,1,512]{2,1,0:T(1,128)S(1)}, f32[2,1,512]{2,1,0:T(1,128)S(1)}, u32[]{:S(2)}, u32[]{:S(2)}) collective-permute-start(f32[2,1,512]{2,1,0:T(1,128)S(1)} %get-tuple-element.81), channel_id=1, source_target_pairs={{8,0},{0,8},{9,1},{1,9},{10,2},{2,10},{11,3},{3,11},{12,4},{4,12},... | collective-permute-start | bytes 12296 | tf_op jit(solution)/shard_map/ppermute | solution.py:18
  248.8 25.1 %collective-permute-start.5 = (f32[2,1,512]{2,1,0:T(1,128)S(1)}, f32[2,1,512]{2,1,0:T(1,128)S(1)}, u32[]{:S(2)}, u32[]{:S(2)}) collective-permute-start(f32[2,1,512]{2,1,0:T(1,128)S(1)} %get-tuple-element.82), channel_id=1, source_target_pairs={{0,8},{8,0},{1,9},{9,1},{2,10},{10,2},{3,11},{11,3},{4,12},{12,4},... | collective-permute-start | bytes 12296 | tf_op jit(solution)/shard_map/ppermute | solution.py:17
  270.3 5.2 collective-permute-start.35
  271.7 5.1 collective-permute-start.36
  274.1 4.0 collective-permute-start.6
  274.1 7.1 %collective-permute-start.7 = (f32[2,258,1]{2,1,0:T(8,128)S(1)}, f32[2,258,1]{2,1,0:T(8,128)S(1)}, u32[]{:S(2)}, u32[]{:S(2)}) collective-permute-start(f32[2,258,1]{2,1,0:T(8,128)S(1)} %get-tuple-element.27), channel_id=1, source_target_pairs={{0,1},{1,2},{2,3},{3,4},{4,5},{5,6},{6,7},{7,0},{8,9},{9,10},{10,1... | collective-permute-start | bytes 6200 | tf_op jit(solution)/shard_map/ppermute | solution.py:17
  277.0 4.2 collective-permute-start.37
  277.2 7.1 %collective-permute-start.38 = (f32[2,258,1]{2,1,0:T(8,128)S(1)}, f32[2,258,1]{2,1,0:T(8,128)S(1)}, u32[]{:S(2)}, u32[]{:S(2)}) collective-permute-start(f32[2,258,1]{2,1,0:T(8,128)S(1)} %get-tuple-element.26), channel_id=1, source_target_pairs={{0,1},{1,2},{2,3},{3,4},{4,5},{5,6},{6,7},{7,0},{8,9},{9,10},{10,1... | collective-permute-start | bytes 6200 | tf_op jit(solution)/shard_map/ppermute | solution.py:17
  289.8 25.6 %collective-permute-start.39 = (f32[2,256,512]{2,1,0:T(8,128)S(1)}, f32[2,256,512]{2,1,0:T(8,128)}, u32[]{:S(2)}, u32[]{:S(2)}) collective-permute-start(f32[2,256,512]{2,1,0:T(8,128)S(1)} %get-tuple-element.5), channel_id=1, source_target_pairs={{0,128},{16,144},{32,160},{48,176},{64,192},{80,208},{96,224},{112... | collective-permute-start | bytes 3145736 | tf_op jit(solution)/shard_map/ppermute | solution.py:26
  316.8 5.2 collective-permute-start.40
  319.2 5.3 collective-permute-start.41
  324.6 4.0 collective-permute-start.42
  324.7 7.1 %collective-permute-start.43 = (f32[2,258,1]{2,1,0:T(8,128)S(1)}, f32[2,258,1]{2,1,0:T(8,128)S(1)}, u32[]{:S(2)}, u32[]{:S(2)}) collective-permute-start(f32[2,258,1]{2,1,0:T(8,128)S(1)} %get-tuple-element.23), channel_id=1, source_target_pairs={{0,1},{1,2},{2,3},{3,4},{4,5},{5,6},{6,7},{7,0},{8,9},{9,10},{10,1... | collective-permute-start | bytes 6200 | tf_op jit(solution)/shard_map/ppermute | solution.py:17
  335.0 53.5 %collective-permute-start.44 = (f32[2,256,512]{2,1,0:T(8,128)}, f32[2,256,512]{2,1,0:T(8,128)}, u32[]{:S(2)}, u32[]{:S(2)}) collective-permute-start(f32[2,256,512]{2,1,0:T(8,128)} %fusion.86), channel_id=1, source_target_pairs={{0,64},{16,80},{32,96},{48,112},{64,128},{80,144},{96,160},{112,17... | collective-permute-start | bytes 3145736 | tf_op jit(solution)/shard_map/ppermute | solution.py:26
  389.9 5.2 collective-permute-start.45
  391.3 5.1 collective-permute-start.46
  396.6 4.0 collective-permute-start.47
  396.6 7.1 %collective-permute-start.48 = (f32[2,258,1]{2,1,0:T(8,128)S(1)}, f32[2,258,1]{2,1,0:T(8,128)S(1)}, u32[]{:S(2)}, u32[]{:S(2)}) collective-permute-start(f32[2,258,1]{2,1,0:T(8,128)S(1)} %get-tuple-element.21), channel_id=1, source_target_pairs={{0,1},{1,2},{2,3},{3,4},{4,5},{5,6},{6,7},{7,0},{8,9},{9,10},{10,1... | collective-permute-start | bytes 6200 | tf_op jit(solution)/shard_map/ppermute | solution.py:17
  408.0 51.0 %collective-permute-start.49 = (f32[2,256,512]{2,1,0:T(8,128)}, f32[2,256,512]{2,1,0:T(8,128)}, u32[]{:S(2)}, u32[]{:S(2)}) collective-permute-start(f32[2,256,512]{2,1,0:T(8,128)} %fusion.66), channel_id=1, source_target_pairs={{0,32},{16,48},{32,64},{48,80},{64,96},{80,112},{96,128},{112,144}... | collective-permute-start | bytes 3145736 | tf_op jit(solution)/shard_map/ppermute | solution.py:26
  460.5 5.2 collective-permute-start.50
  461.3 5.1 collective-permute-start.51
  466.6 4.3 collective-permute-start.52
  466.9 7.1 %collective-permute-start.53 = (f32[2,258,1]{2,1,0:T(8,128)S(1)}, f32[2,258,1]{2,1,0:T(8,128)S(1)}, u32[]{:S(2)}, u32[]{:S(2)}) collective-permute-start(f32[2,258,1]{2,1,0:T(8,128)S(1)} %get-tuple-element.19), channel_id=1, source_target_pairs={{0,1},{1,2},{2,3},{3,4},{4,5},{5,6},{6,7},{7,0},{8,9},{9,10},{10,1... | collective-permute-start | bytes 6200 | tf_op jit(solution)/shard_map/ppermute | solution.py:17
  477.5 26.8 %collective-permute-start.54 = (f32[2,256,512]{2,1,0:T(8,128)S(1)}, f32[2,256,512]{2,1,0:T(8,128)S(1)}, u32[]{:S(2)}, u32[]{:S(2)}) collective-permute-start(f32[2,256,512]{2,1,0:T(8,128)S(1)} %fusion.47), channel_id=1, source_target_pairs={{0,16},{16,32},{32,48},{48,64},{64,80},{80,96},{96,112},{112,128},... | collective-permute-start | bytes 3145736 | tf_op jit(solution)/shard_map/ppermute | solution.py:26
  504.5 5.2 collective-permute-start.55
  508.0 5.1 collective-permute-start.56
  513.3 4.0 collective-permute-start.57
  513.3 7.1 %collective-permute-start.58 = (f32[2,258,1]{2,1,0:T(8,128)S(1)}, f32[2,258,1]{2,1,0:T(8,128)S(1)}, u32[]{:S(2)}, u32[]{:S(2)}) collective-permute-start(f32[2,258,1]{2,1,0:T(8,128)S(1)} %get-tuple-element.17), channel_id=1, source_target_pairs={{0,1},{1,2},{2,3},{3,4},{4,5},{5,6},{6,7},{7,0},{8,9},{9,10},{10,1... | collective-permute-start | bytes 6200 | tf_op jit(solution)/shard_map/ppermute | solution.py:17
  522.6 27.6 %collective-permute-start.59 = (f32[2,256,512]{2,1,0:T(8,128)S(1)}, f32[2,256,512]{2,1,0:T(8,128)S(1)}, u32[]{:S(2)}, u32[]{:S(2)}) collective-permute-start(f32[2,256,512]{2,1,0:T(8,128)S(1)} %fusion.28), channel_id=1, source_target_pairs={{0,16},{16,32},{32,48},{48,64},{64,80},{80,96},{96,112},{112,128},... | collective-permute-start | bytes 3145736 | tf_op jit(solution)/shard_map/ppermute | solution.py:26
  550.5 5.2 collective-permute-start.60
  550.7 5.1 collective-permute-start.61
  555.9 4.0 collective-permute-start.62
  555.9 7.1 %collective-permute-start.63 = (f32[2,258,1]{2,1,0:T(8,128)S(1)}, f32[2,258,1]{2,1,0:T(8,128)S(1)}, u32[]{:S(2)}, u32[]{:S(2)}) collective-permute-start(f32[2,258,1]{2,1,0:T(8,128)S(1)} %get-tuple-element.15), channel_id=1, source_target_pairs={{0,1},{1,2},{2,3},{3,4},{4,5},{5,6},{6,7},{7,0},{8,9},{9,10},{10,1... | collective-permute-start | bytes 6200 | tf_op jit(solution)/shard_map/ppermute | solution.py:17
  (15 other events, 242.9 us)
where the time goes:
time: 577 us; the launch traced here: 567 us
  waiting for transfers between devices  398 us (69%)
  starting transfers between devices  113 us (20%)
  other arithmetic  54 us (9%)
    ppermute x12, waiting for transfers between devices, shifted(): return lax.ppermute(block, axis, route)  305 us
    ppermute x26, waiting for transfers between devices, padded_2(): before = lax.ppermute(last, axis, up)  57 us
    ppermute x26, starting transfers between devices, padded_2(): after = lax.ppermute(leading, axis, down)  45.5 us
    ppermute x12, starting transfers between devices, shifted(): return lax.ppermute(block, axis, route)  37.3 us
    ppermute x26, waiting for transfers between devices, padded_2(): after = lax.ppermute(leading, axis, down)  36.1 us
    ppermute x26, starting transfers between devices, padded_2(): before = lax.ppermute(last, axis, up)  29.8 us
    select_n x3, other arithmetic, descend(): relaxed = jnp.where(relax_here, image_prior + level_rhs, values)  16.2 us
  transfers between devices with their start and end apart: 64, of which 51 were waited for; matrix products, arithmetic and copies ran while one was open for 4% of the time, Pallas kernels for 0%

commit v1 on v0

v1 whole, which is shorter than its diff:
```python
import jax
import jax.numpy as jnp
from jax import lax
from jax.experimental import pallas as pl
from jax.experimental.pallas import tpu as pltpu
from jax.sharding import PartitionSpec as P

VISCOSITY = 0.5
COURANT = 0.7
MESH = pl.DeviceIdType.MESH
NT = 16
ROWS = 16
COLS = 512
TILES = COLS // 128
STEP = COURANT / (NT * (2.0 + 4.0 * VISCOSITY))
BATCH = (16, 16, 8, 4, 3, 3, 4, 3, 1)
NB = len(BATCH)


def slab_of(t):
    return jnp.where(t < 8, t, 23 - t)


def kernel(initial, forcing, guess, out, *scratch):
    (S, F, R0, T1, G1, G2, G3, G4, Fx, U, O, col_out, col_in) = scratch[:13]
    row_out = scratch[13 : 13 + NB]
    row_in = scratch[13 + NB : 13 + 2 * NB]
    local_sem, fwd_send, fwd_recv, halo_send, halo_recv, ret_send, ret_recv, ret_local = scratch[13 + 2 * NB :]

    me = lax.axis_index("tm")
    sx = lax.axis_index("sx")
    sy = lax.axis_index("sy")
    slab = slab_of(me)
    above = {"tm": slab_of(lax.rem(slab + 1, 16)), "sx": jnp.where(slab == 15, 1 - sx, sx)}
    below = {"tm": slab_of(lax.rem(slab + 15, 16)), "sx": jnp.where(slab == 0, 1 - sx, sx)}
    right = {"sy": lax.rem(sy + 1, 8)}
    left = {"sy": lax.rem(sy + 7, 8)}
    sides = (above, below, right, left)

    def rows_of(t):
        return pl.ds(pl.multiple_of(slab_of(t) * ROWS, ROWS), ROWS)

    own_rows = rows_of(me)

    barrier = pltpu.get_barrier_semaphore()

    def greet(d, c):
        pl.semaphore_signal(barrier, inc=1, device_id={"tm": lax.rem(me + d, NT)}, device_id_type=MESH)
        return c

    lax.fori_loop(1, NT, greet, 0)
    for side in sides:
        pl.semaphore_signal(barrier, inc=1, device_id=side, device_id_type=MESH)

    stage_in = [
        pltpu.make_async_copy(initial.at[:, own_rows, :], S.at[0], local_sem.at[0]),
        pltpu.make_async_copy(forcing.at[:, own_rows, :], F, local_sem.at[1]),
        pltpu.make_async_copy(guess.at[0, :, own_rows, :], S.at[me + 1], local_sem.at[2]),
    ]
    for copy in stage_in:
        copy.start()
    pl.semaphore_wait(barrier, NT - 1 + 4)

    def forward(peer):
        return pltpu.make_async_remote_copy(
            src_ref=guess.at[0, :, rows_of(peer), :],
            dst_ref=S.at[me + 1],
            send_sem=fwd_send.at[peer],
            recv_sem=fwd_recv.at[me],
            device_id={"tm": peer},
            device_id_type=MESH,
        )

    def forwarded(peer):
        return pltpu.make_async_remote_copy(
            src_ref=guess.at[0, :, own_rows, :],
            dst_ref=S.at[peer + 1],
            send_sem=fwd_send.at[peer],
            recv_sem=fwd_recv.at[peer],
            device_id={"tm": peer},
            device_id_type=MESH,
        )

    def start_forward(d, c):
        forward(lax.rem(me + d, NT)).start()
        return c

    lax.fori_loop(1, NT, start_forward, 0)
    for copy in stage_in:
        copy.wait()

    lane = lax.broadcasted_iota(jnp.int32, (ROWS, 128), 1)
    row = lax.broadcasted_iota(jnp.int32, (ROWS, 128), 0)
    blank = jnp.zeros((ROWS, 128), jnp.float32)

    def lanes(j):
        return slice(128 * j, 128 * (j + 1))

    def halo_copies(b):
        copies = []
        for i, side in enumerate(sides):
            src, dst = ((row_out[b], row_in[b]) if i < 2 else (col_out.at[b], col_in.at[b]))
            copies.append(
                pltpu.make_async_remote_copy(
                    src_ref=src.at[i % 2],
                    dst_ref=dst.at[i % 2],
                    send_sem=halo_send.at[b, i],
                    recv_sem=halo_recv.at[b, i],
                    device_id=side,
                    device_id_type=MESH,
                )
            )
        return copies

    def send_halo(b, packed):
        col_out[b, 0] = packed[0]
        col_out[b, 1] = packed[1]
        for copy in halo_copies(b):
            copy.start()

    def wait_halo(b):
        for copy in halo_copies(b):
            copy.wait_recv()

    def pack(b, i, c, j, w, packed):
        row_out[b][0, i, c : c + 1, lanes(j)] = w[ROWS - 1 : ROWS]
        row_out[b][1, i, c : c + 1, lanes(j)] = w[0:1]
        index = 2 * i + c
        last, first = packed
        if j == TILES - 1:
            last = jnp.where(lane == index, pltpu.roll(w, index + 1, 1), last)
        if j == 0:
            first = jnp.where(lane == index, pltpu.roll(w, index, 1), first)
        return last, first

    def rates(source, k, b, i):
        w = [[source[k, c, :, lanes(j)] for c in range(2)] for j in range(TILES)]
        up = [[pltpu.roll(w[j][c], 1, 1) for c in range(2)] for j in range(TILES)]
        down = [[pltpu.roll(w[j][c], 127, 1) for c in range(2)] for j in range(TILES)]
        before = [pltpu.roll(col_in[b, 0], 128 - (2 * i + c), 1) for c in range(2)]
        after = [pltpu.roll(col_in[b, 1], 127 - (2 * i + c), 1) for c in range(2)]
        result = []
        for j in range(TILES):
            first, second = w[j]
            east_w = 0.5 - jnp.minimum(first, 0.0)
            west_w = 0.5 + jnp.maximum(first, 0.0)
            north_w = 0.5 - jnp.minimum(second, 0.0)
            south_w = 0.5 + jnp.maximum(second, 0.0)
            pair = []
            for c in range(2):
                x = w[j][c]
                west = jnp.where(row == 0, row_in[b][0, i, c : c + 1, lanes(j)], pltpu.roll(x, 1, 0))
                east = jnp.where(row == ROWS - 1, row_in[b][1, i, c : c + 1, lanes(j)], pltpu.roll(x, ROWS - 1, 0))
                south = jnp.where(lane == 0, up[j - 1][c] if j > 0 else before[c], up[j][c])
                north = jnp.where(lane == 127, down[j + 1][c] if j < TILES - 1 else after[c], down[j][c])
                pair.append(
                    west_w * (west - x)
                    + east_w * (east - x)
                    + south_w * (south - x)
                    + north_w * (north - x)
                    + F[c, :, lanes(j)]
                )
            result.append(pair)
        return w, result

    def each():
        return [(j, c) for j in range(TILES) for c in range(2)]

    def at(ref, k, c, j):
        return ref[k, c, :, lanes(j)]

    def put(ref, k, c, j, value):
        ref[k, c, :, lanes(j)] = value

    def send_back(slot, k, source):
        @pl.when(me == k)
        def _():
            pltpu.make_async_copy(source, out.at[slot, :, own_rows, :], ret_local.at[slot]).start()

        @pl.when(me != k)
        def _():
            back(slot, k, source).start()

    def back(slot, k, source):
        return pltpu.make_async_remote_copy(
            src_ref=source,
            dst_ref=out.at[slot, :, own_rows, :],
            send_sem=ret_send.at[slot, k],
            recv_sem=ret_recv.at[slot, me],
            device_id={"tm": k},
            device_id_type=MESH,
        )

    def arrive(k, packed):
        @pl.when(jnp.logical_and(k > 0, k - 1 != me))
        def _():
            forwarded(k - 1).wait_recv()

        for j, c in each():
            packed = pack(0, k, c, j, at(S, k, c, j), packed)
        return packed

    send_halo(0, lax.fori_loop(0, 16, arrive, (blank, blank)))

    @pl.when(me != 15)
    def _():
        forwarded(15).wait_recv()

    wait_halo(0)

    def first_step(k, packed):
        w, rate = rates(S, k, 0, k)
        for j, c in each():
            put(R0, k, c, j, rate[j][c])
            new = w[j][c] + STEP * rate[j][c]
            put(T1, k, c, j, new)
            packed = pack(1, k, c, j, new, packed)
        return packed

    send_halo(1, lax.fori_loop(0, 16, first_step, (blank, blank)))
    send_back(0, 0, T1.at[0])
    wait_halo(1)

    def coarse_rhs(g, point, image, base):
        residual = g - (point - image)
        return residual + point - base

    def second_step(m, packed):
        for odd in range(2):
            k = 2 * m + odd
            w, rate = rates(T1, k, 1, k)
            for j, c in each():
                base = at(S, k, c, j) + 2 * STEP * at(R0, k, c, j)
                g = coarse_rhs(0.0, at(S, k + 1, c, j), w[j][c] + STEP * rate[j][c], base)
                put(G1, k + 1, c, j, g)
                if not odd:
                    relaxed = base + g
                    put(Fx, k + 1, c, j, relaxed)
                    packed = pack(2, m, c, j, relaxed, packed)
        return packed

    send_halo(2, lax.fori_loop(0, 8, second_step, (blank, blank)))
    send_back(1, 0, Fx.at[1])
    wait_halo(2)

    def third_step(q, packed):
        for odd in range(2):
            m = 2 * q + odd
            k = 2 * m
            w, rate = rates(Fx, k + 1, 2, m)
            for j, c in each():
                base = at(S, k, c, j) + 4 * STEP * at(R0, k, c, j)
                g = coarse_rhs(at(G1, k + 2, c, j), at(S, k + 2, c, j), w[j][c] + 2 * STEP * rate[j][c], base)
                put(G2, m + 1, c, j, g)
                if not odd:
                    put(O, k + 1, c, j, w[j][c] + STEP * rate[j][c])
                    relaxed = base + g
                    put(Fx, k + 2, c, j, relaxed)
                    packed = pack(3, q, c, j, relaxed, packed)
        return packed

    send_halo(3, lax.fori_loop(0, 4, third_step, (blank, blank)))
    send_back(0, 1, O.at[1])
    send_back(1, 1, Fx.at[2])
    wait_halo(3)

    packed = (blank, blank)
    for q in range(4):
        k = 4 * q
        w, rate = rates(Fx, k + 2, 3, q)
        for j, c in each():
            base = at(S, k, c, j) + 8 * STEP * at(R0, k, c, j)
            g = coarse_rhs(at(G2, 2 * q + 2, c, j), at(S, k + 4, c, j), w[j][c] + 4 * STEP * rate[j][c], base)
            put(G3, q + 1, c, j, g)
            if q % 2 == 0:
                relaxed = base + g
                put(Fx, k + 4, c, j, relaxed)
                packed = pack(4, q // 2, c, j, relaxed, packed)
            if q == 0:
                put(O, 2, c, j, w[j][c] + STEP * rate[j][c])
                new = w[j][c] + 2 * STEP * rate[j][c] + at(G1, 3, c, j)
                put(U, 3, c, j, new)
                packed = pack(4, 2, c, j, new, packed)
    send_halo(4, packed)
    send_back(0, 2, O.at[2])
    send_back(1, 2, U.at[3])
    send_back(1, 3, Fx.at[4])
    wait_halo(4)

    packed = (blank, blank)
    for q in range(2):
        k = 8 * q
        w, rate = rates(Fx, k + 4, 4, q)
        for j, c in each():
            base = at(S, k, c, j) + 16 * STEP * at(R0, k, c, j)
            g = coarse_rhs(at(G3, 2 * q + 2, c, j), at(S, k + 8, c, j), w[j][c] + 8 * STEP * rate[j][c], base)
            if q == 1:
                put(G4, 0, c, j, g)
                continue
            new = base + g
            put(U, 8, c, j, new)
            packed = pack(5, 0, c, j, new, packed)
            put(O, 4, c, j, w[j][c] + STEP * rate[j][c])
            new = w[j][c] + 4 * STEP * rate[j][c] + at(G2, 3, c, j)
            put(U, 6, c, j, new)
            packed = pack(5, 1, c, j, new, packed)
            new = w[j][c] + 2 * STEP * rate[j][c] + at(G1, 5, c, j)
            put(U, 5, c, j, new)
            packed = pack(5, 2, c, j, new, packed)
        if q == 0:
            send_halo(5, packed)
    w, rate = rates(U, 3, 4, 2)
    for j, c in each():
        put(O, 3, c, j, w[j][c] + STEP * rate[j][c])
    for slot, k in ((0, 4), (1, 7), (1, 5), (1, 4), (0, 3)):
        send_back(slot, k, O.at[k] if slot == 0 else U.at[k + 1])

    def ascend(k, b, i, targets, packed):
        w, rate = rates(U, k, b, i)
        for j, c in each():
            put(O, k, c, j, w[j][c] + STEP * rate[j][c])
            for point, factor, (right_side, index), place in targets:
                new = w[j][c] + factor * STEP * rate[j][c] + at(right_side, index, c, j)
                put(U, point, c, j, new)
                if place is not None:
                    packed = pack(b + 1, place, c, j, new, packed)
        return packed

    plan = (
        (
            5,
            (
                (8, 0, ((12, 8, (G3, 3), 0), (10, 4, (G2, 5), 1), (9, 2, (G1, 9), 2), (16, 16, (G4, 0), None))),
                (6, 1, ((7, 2, (G1, 7), 3),)),
                (5, 2, ()),
            ),
        ),
        (
            6,
            (
                (12, 0, ((14, 4, (G2, 7), 0), (13, 2, (G1, 13), 1))),
                (10, 1, ((11, 2, (G1, 11), 2),)),
                (9, 2, ()),
                (7, 3, ()),
            ),
        ),
        (7, ((14, 0, ((15, 2, (G1, 15), 0),)), (13, 1, ()), (11, 2, ()))),
        (8, ((15, 0, ()),)),
    )
    for b, fields in plan:
        wait_halo(b)
        packed = (blank, blank)
        for k, i, targets in fields:
            packed = ascend(k, b, i, targets, packed)
        if b + 1 < NB:
            send_halo(b + 1, packed)
        for k, i, targets in fields:
            send_back(0, k, O.at[k])
            for target in targets:
                send_back(1, target[0] - 1, U.at[target[0]])

    for b in range(NB):
        for copy in halo_copies(b):
            copy.wait_send()

    def finish(peer, c):
        @pl.when(peer != me)
        def _():
            forward(peer).wait_send()
            for slot in range(2):
                back(slot, peer, O.at[0]).wait_send()
                pltpu.make_async_remote_copy(
                    src_ref=O.at[0],
                    dst_ref=out.at[slot, :, rows_of(peer), :],
                    send_sem=ret_send.at[slot, peer],
                    recv_sem=ret_recv.at[slot, peer],
                    device_id={"tm": peer},
                    device_id_type=MESH,
                ).wait_recv()

        return c

    lax.fori_loop(0, NT, finish, 0)
    for slot in range(2):
        pltpu.make_async_copy(O.at[0], out.at[slot, :, own_rows, :], ret_local.at[slot]).wait()


def body(initial, forcing, guess):
    def field(n):
        return pltpu.VMEM((n, 2, ROWS, COLS), jnp.float32)

    scratch = [
        field(17),
        pltpu.VMEM((2, ROWS, COLS), jnp.float32),
        field(16),
        field(16),
        field(17),
        field(9),
        field(5),
        field(1),
        field(17),
        field(17),
        field(16),
        pltpu.VMEM((NB, 2, ROWS, 128), jnp.float32),
        pltpu.VMEM((NB, 2, ROWS, 128), jnp.float32),
    ]
    for _ in range(2):
        scratch += [pltpu.VMEM((2, n, 2, COLS), jnp.float32) for n in BATCH]
    dma = pltpu.SemaphoreType.DMA
    scratch += [dma((3,)), dma((NT,)), dma((NT,)), dma((NB, 4)), dma((NB, 4)), dma((2, NT)), dma((2, NT)), dma((2,))]
    spec = pl.BlockSpec(memory_space=pl.ANY)
    return pl.pallas_call(
        kernel,
        out_shape=jax.ShapeDtypeStruct((2, 2, 256, COLS), jnp.float32),
        in_specs=[spec] * 3,
        out_specs=spec,
        scratch_shapes=scratch,
        compiler_params=pltpu.CompilerParams(
            collective_id=0, has_side_effects=True, vmem_limit_bytes=48 * 1024 * 1024
        ),
        name="cycle",
    )(initial, forcing, guess)


def solution(mesh):
    in_specs = (P(None, "sx", "sy"), P(None, "sx", "sy"), P("tm", None, "sx", "sy"))
    out_specs = P("tm", None, "sx", "sy")
    return jax.shard_map(body, mesh=mesh, in_specs=in_specs, out_specs=out_specs, check_vma=False)
```

time: 577 us -> 124 us (0.21); the launches traced: 567 us -> 123 us
  waiting for transfers between devices: 398 us -> 0 us
  Pallas kernels: 0 us -> 118 us
  starting transfers between devices: 113 us -> 0 us
  other arithmetic: 54 us -> 0 us
    ppermute x64 -> x0, waiting for transfers between devices: 398 us -> none  [the longest x12 305 us: shifted(): return lax.ppermute(block, axis, route)]
    pallas_call x0 -> x1, Pallas kernels: none -> 118 us  [body(): pl.pallas_call(kernel, out_shape=jax.ShapeDtypeStruct((2, 2, 256, COLS),...]
    ppermute x64 -> x0, starting transfers between devices: 113 us -> none  [the longest x26 45.5 us: padded_2(): after = lax.ppermute(leading, axis, down)]
    select_n x13 -> x0, other arithmetic: 34.3 us -> none  [the longest x3 16.2 us: descend(): relaxed = jnp.where(relax_here, image_prior + level_rhs, values)]
    add x2 -> x0, other arithmetic: 8.33 us -> none  [the longest x1 5.49 us: descend(): first_point = image_prior + level_rhs]
  transfers between devices with their start and end apart: 64 -> 0, of which waited for: 51 -> 0; matrix products, arithmetic and copies ran while one was open for 4% -> 0% of each run, Pallas kernels for 0% -> 0%
where the time goes in v1:
time: 124 us; the launch traced here: 123 us
  Pallas kernels  118 us (95%)
  local copies, waits for them, and re-layouts  4.99 us (4%)
    pallas_call x1, Pallas kernels, body(): pl.pallas_call(kernel, out_shape=jax.ShapeDtypeStruct((2, 2, 256, COLS),...  118 us
    unnamed x7, local copies, waits for them, and re-layouts  4.99 us

profile of v1, /device:TPU:2, one launch (start us, length us, event | category | flops | bytes accessed | tf_op | source)
XLA Modules:
  0.0 122.5 jit_solution(10964706247281862340)
XLA Ops:
  0.0 0.0 copy-start
  0.0 1.2 copy-done
  1.2 0.0 copy-start.1
  1.2 1.2 copy-done.1
  2.5 0.0 copy-start.2
  2.5 1.2 copy-done.2
  3.7 117.5 %cycle.1 = f32[2,2,256,512]{3,2,1,0:T(8,128)S(1)} custom-call(f32[2,256,512]{2,1,0:T(8,128)S(1)} %copy-done, f32[2,256,512]{2,1,0:T(8,128)S(1)} %copy-done.1, f32[1,2,256,512]{3,2,1,0:T(8,128)S(1)} %copy-done.2), custom_call_target="tpu_custom_call" | custom-call | tf_op jit(solution)/shard_map/cycle/pallas_call | solution.py:412
  121.2 1.3 %copy.5 = f32[2,2,256,512]{3,2,1,0:T(8,128)} copy(f32[2,2,256,512]{3,2,1,0:T(8,128)S(1)} %cycle.1) | data formatting | bytes 4194304
Async XLA Ops:
  0.0 1.2 copy-start
  1.2 1.2 copy-start.1
  2.5 1.2 copy-start.2

commit v2 on v0

v2 whole, which is shorter than its diff:
```python
import jax
import jax.numpy as jnp
from jax import lax
from jax.experimental import pallas as pl
from jax.experimental.pallas import tpu as pltpu
from jax.sharding import PartitionSpec as P

VISCOSITY = 0.5
COURANT = 0.7
MESH = pl.DeviceIdType.MESH
NT = 16
BLOCK_ROWS, BLOCK_COLS = 256, 512
ROWS, COLS = 32, 256
HALO = 4
HELD_ROWS, HELD_COLS = ROWS + 2 * HALO, COLS + 128
TILES = HELD_COLS // 128
STEP = COURANT / (NT * (2.0 + 4.0 * VISCOSITY))
BATCH = (2, 8, 7, 2, 2)
NB = len(BATCH)
UP, DOWN, RIGHT, LEFT, UP_RIGHT, DOWN_RIGHT, UP_LEFT, DOWN_LEFT = range(8)


def kernel(initial, forcing, guess, out, *scratch):
    (S, F, R0, T1, G1, G2, G3, G4, Fx, U, prior, final, col_out, col_in, corner_in, wide) = scratch[:16]
    (edge_row_out, edge_row_in, edge_col_out, edge_col_in) = scratch[16:20]
    row_out = scratch[20 : 20 + NB]
    row_in = scratch[20 + NB : 20 + 2 * NB]
    (local_sem, fwd_send, fwd_recv, halo_send, halo_recv, ret_send, ret_recv, ret_local, edge_send, edge_recv, final_sem) = (
        scratch[20 + 2 * NB :]
    )

    me = lax.axis_index("tm")
    sx = lax.axis_index("sx")
    sy = lax.axis_index("sy")
    xl = me // 8
    z = lax.rem(me, 8)

    def mirrored(i):
        return jnp.where(sx == 0, i, 7 - i)

    zz = mirrored(z)

    def beside(vertical, horizontal):
        if vertical == 0:
            nz, nsx = z, sx
        elif vertical == 1:
            nz, nsx = jnp.where(zz < 7, mirrored(zz + 1), z), jnp.where(zz < 7, sx, 1 - sx)
        else:
            nz, nsx = jnp.where(zz > 0, mirrored(zz - 1), z), jnp.where(zz > 0, sx, 1 - sx)
        if horizontal == 0:
            nx, nsy = xl, sy
        elif horizontal == 1:
            nx, nsy = 1 - xl, jnp.where(xl == 0, sy, lax.rem(sy + 1, 8))
        else:
            nx, nsy = 1 - xl, jnp.where(xl == 1, sy, lax.rem(sy + 7, 8))
        return {"tm": nx * 8 + nz, "sx": nsx, "sy": nsy}

    sides = [beside(*v) for v in ((1, 0), (-1, 0), (0, 1), (0, -1), (1, 1), (-1, 1), (1, -1), (-1, -1))]
    block_sides = [{"sx": 1 - sx}, {"sy": lax.rem(sy + 1, 8)}, {"sy": lax.rem(sy + 7, 8)}]

    def rows_of(t):
        return pl.ds(pl.multiple_of(mirrored(lax.rem(t, 8)) * ROWS, ROWS), ROWS)

    def cols_of(t):
        return pl.ds(pl.multiple_of((t // 8) * COLS, COLS), COLS)

    own_rows, own_cols = rows_of(me), cols_of(me)

    def prior_rows(t):
        return pl.ds(pl.multiple_of(8 + mirrored(lax.rem(t, 8)) * ROWS, 8), ROWS)

    def core(ref, k):
        return ref.at[k, :, 0:ROWS, 0:COLS]

    barrier = pltpu.get_barrier_semaphore()

    def greet(d, c):
        pl.semaphore_signal(barrier, inc=1, device_id={"tm": lax.rem(me + d, NT)}, device_id_type=MESH)
        return c

    lax.fori_loop(1, NT, greet, 0)
    for side in sides + block_sides:
        pl.semaphore_signal(barrier, inc=1, device_id=side, device_id_type=MESH)

    stage_in = [
        pltpu.make_async_copy(initial.at[:, own_rows, own_cols], core(S, 0), local_sem.at[0]),
        pltpu.make_async_copy(forcing.at[:, own_rows, own_cols], core(F, 0), local_sem.at[1]),
        pltpu.make_async_copy(guess.at[0, :, own_rows, own_cols], core(S, me + 1), local_sem.at[2]),
    ]
    for copy in stage_in:
        copy.start()
    pl.semaphore_wait(barrier, NT - 1 + 8 + 3)

    def forward(peer):
        return pltpu.make_async_remote_copy(
            src_ref=guess.at[0, :, rows_of(peer), cols_of(peer)],
            dst_ref=core(S, me + 1),
            send_sem=fwd_send.at[peer],
            recv_sem=fwd_recv.at[me],
            device_id={"tm": peer},
            device_id_type=MESH,
        )

    def forwarded(peer):
        return pltpu.make_async_remote_copy(
            src_ref=guess.at[0, :, own_rows, own_cols],
            dst_ref=core(S, peer + 1),
            send_sem=fwd_send.at[peer],
            recv_sem=fwd_recv.at[peer],
            device_id={"tm": peer},
            device_id_type=MESH,
        )

    def start_forward(d, c):
        forward(lax.rem(me + d, NT)).start()
        return c

    lax.fori_loop(1, NT, start_forward, 0)

    lane = lax.broadcasted_iota(jnp.int32, (HELD_ROWS, 128), 1)
    core_lane = lax.broadcasted_iota(jnp.int32, (ROWS, 128), 1)
    blank = jnp.zeros((ROWS, 128), jnp.float32)

    def lanes(j):
        return slice(128 * j, 128 * (j + 1))

    def halo_copies(b):
        parts = (
            (UP, row_out[b].at[0], row_in[b].at[1]),
            (DOWN, row_out[b].at[1], row_in[b].at[0]),
            (RIGHT, col_out.at[b, 0], col_in.at[b, 0]),
            (LEFT, col_out.at[b, 1], col_in.at[b, 1]),
            (DOWN_RIGHT, col_out.at[b, 0, 0:8], corner_in.at[b, 0, 0]),
            (UP_RIGHT, col_out.at[b, 0, ROWS - 8 : ROWS], corner_in.at[b, 0, 1]),
            (DOWN_LEFT, col_out.at[b, 1, 0:8], corner_in.at[b, 1, 0]),
            (UP_LEFT, col_out.at[b, 1, ROWS - 8 : ROWS], corner_in.at[b, 1, 1]),
        )
        return [
            pltpu.make_async_remote_copy(
                src_ref=src,
                dst_ref=dst,
                send_sem=halo_send.at[b, i],
                recv_sem=halo_recv.at[b, i],
                device_id=sides[to],
                device_id_type=MESH,
            )
            for i, (to, src, dst) in enumerate(parts)
        ]

    def pack(ref, k, b, i, packed):
        last, first = packed
        for c in range(2):
            row_out[b][0, i, c] = ref[k, c, ROWS - HALO : ROWS, 0:COLS]
            row_out[b][1, i, c] = ref[k, c, 0:HALO, 0:COLS]
            index = 8 * i + HALO * c
            mine = jnp.logical_and(core_lane >= index, core_lane < index + HALO)
            tail = ref[k, c, 0:ROWS, COLS - 128 : COLS]
            head = ref[k, c, 0:ROWS, 0:128]
            last = jnp.where(mine, pltpu.roll(tail, lax.rem(index + HALO, 128), 1), last)
            first = jnp.where(mine, pltpu.roll(head, index, 1), first)
        return last, first

    def send_halo(b, packed):
        col_out[b, 0] = packed[0]
        col_out[b, 1] = packed[1]
        for copy in halo_copies(b):
            copy.start()

    def wait_halo(b):
        for copy in halo_copies(b):
            copy.wait_recv()
        for side in range(2):
            wide[b, side, 0:ROWS] = col_in[b, side]
            wide[b, side, ROWS : ROWS + HALO] = corner_in[b, side, 0, 0:HALO]
            wide[b, side, ROWS + HALO : HELD_ROWS] = corner_in[b, side, 1, HALO:8]

    def unpack(ref, k, b, i):
        for c in range(2):
            ref[k, c, ROWS : ROWS + HALO, 0:COLS] = row_in[b][0, i, c]
            ref[k, c, ROWS + HALO : HELD_ROWS, 0:COLS] = row_in[b][1, i, c]
            index = 8 * i + HALO * c
            after = pltpu.roll(wide[b, 1], lax.rem(128 - index, 128), 1)
            before = pltpu.roll(wide[b, 0], lax.rem(256 - HALO - index, 128), 1)
            ref[k, c, :, COLS:HELD_COLS] = jnp.where(lane < 64, after, before)

    def slopes(first, second):
        return (
            0.5 + jnp.maximum(first, 0.0),
            0.5 - jnp.minimum(first, 0.0),
            0.5 + jnp.maximum(second, 0.0),
            0.5 - jnp.minimum(second, 0.0),
        )

    def rates(ref, k):
        w = [[ref[k, c, :, lanes(j)] for c in range(2)] for j in range(TILES)]
        up = [[pltpu.roll(w[j][c], 1, 1) for c in range(2)] for j in range(TILES)]
        down = [[pltpu.roll(w[j][c], 127, 1) for c in range(2)] for j in range(TILES)]
        result = []
        for j in range(TILES):
            west_w, east_w, south_w, north_w = slopes(*w[j])
            pair = []
            for c in range(2):
                x = w[j][c]
                west = pltpu.roll(x, 1, 0)
                east = pltpu.roll(x, HELD_ROWS - 1, 0)
                south = jnp.where(lane == 0, up[j - 1][c], up[j][c])
                north = jnp.where(lane == 127, down[(j + 1) % TILES][c], down[j][c])
                pair.append(
                    west_w * (west - x)
                    + east_w * (east - x)
                    + south_w * (south - x)
                    + north_w * (north - x)
                    + F[0, c, :, lanes(j)]
                )
            result.append(pair)
        return w, result

    def each():
        return [(j, c) for j in range(TILES) for c in range(2)]

    def at(ref, k, c, j):
        return ref[k, c, :, lanes(j)]

    def put(ref, k, c, j, value):
        ref[k, c, :, lanes(j)] = value

    def back(slot, k):
        if slot == 0:
            dst, to = out.at[1, :, own_rows, own_cols], k - 1
        else:
            dst, to = prior.at[:, prior_rows(me), own_cols], k
        src = core(U, k)
        remote = pltpu.make_async_remote_copy(
            src_ref=src,
            dst_ref=dst,
            send_sem=ret_send.at[slot, k],
            recv_sem=ret_recv.at[slot, me],
            device_id={"tm": to},
            device_id_type=MESH,
        )
        return to, remote, pltpu.make_async_copy(src, dst, ret_local.at[slot])

    def send_back(slot, k):
        to, remote, local = back(slot, k)

        @pl.when(me == to)
        def _():
            local.start()

        @pl.when(me != to)
        def _():
            remote.start()

    for copy in stage_in:
        copy.wait()
    packed = pack(S, 0, 0, 0, (blank, blank))
    send_halo(0, pack(F, 0, 0, 1, packed))

    def arrive(first, b):
        def one(i, packed):
            k = first + i

            @pl.when(k - 1 != me)
            def _():
                forwarded(k - 1).wait_recv()

            return pack(S, k, b, i, packed)

        return one

    send_halo(1, lax.fori_loop(0, 8, arrive(1, 1), (blank, blank)))
    send_halo(2, lax.fori_loop(0, 7, arrive(9, 2), (blank, blank)))

    @pl.when(me != NT - 1)
    def _():
        forwarded(NT - 1).wait_recv()

    for c in range(2):
        S[NT, c, ROWS:HELD_ROWS, :] = jnp.zeros((HELD_ROWS - ROWS, HELD_COLS), jnp.float32)
        S[NT, c, 0:ROWS, COLS:HELD_COLS] = jnp.zeros((ROWS, 128), jnp.float32)

    wait_halo(0)
    unpack(S, 0, 0, 0)
    unpack(F, 0, 0, 1)

    def coarse_rhs(g, point, image, base):
        residual = g - (point - image)
        return residual + point - base

    def descend(half):
        start = 8 * half

        def fine(k, carry):
            w, rate = rates(S, k)
            for j, c in each():
                put(R0, k, c, j, rate[j][c])
                put(T1, k, c, j, w[j][c] + STEP * rate[j][c])
            w, rate = rates(T1, k)
            for j, c in each():
                base = at(S, k, c, j) + 2 * STEP * at(R0, k, c, j)
                g = coarse_rhs(0.0, at(S, k + 1, c, j), w[j][c] + STEP * rate[j][c], base)
                put(G1, k + 1, c, j, g)
                put(Fx, k + 1, c, j, base + g)
            return carry

        lax.fori_loop(start, start + 8, fine, 0)

        def second(m, carry):
            k = 2 * m
            w, rate = rates(Fx, k + 1)
            for j, c in each():
                base = at(S, k, c, j) + 4 * STEP * at(R0, k, c, j)
                g = coarse_rhs(at(G1, k + 2, c, j), at(S, k + 2, c, j), w[j][c] + 2 * STEP * rate[j][c], base)
                put(G2, m + 1, c, j, g)
                put(Fx, k + 2, c, j, base + g)
            return carry

        lax.fori_loop(start // 2, start // 2 + 4, second, 0)

        for q in (2 * half, 2 * half + 1):
            k = 4 * q
            w, rate = rates(Fx, k + 2)
            for j, c in each():
                base = at(S, k, c, j) + 8 * STEP * at(R0, k, c, j)
                g = coarse_rhs(at(G2, 2 * q + 2, c, j), at(S, k + 4, c, j), w[j][c] + 4 * STEP * rate[j][c], base)
                put(G3, q + 1, c, j, g)
                if q % 2 == 0:
                    put(Fx, k + 4, c, j, base + g)
                if q == 0:
                    put(U, 1, c, j, at(Fx, 1, c, j))
                    put(U, 2, c, j, w[j][c])
                    put(U, 3, c, j, w[j][c] + 2 * STEP * rate[j][c] + at(G1, 3, c, j))
                    put(U, 4, c, j, base + g)

    def exchange(b, fields):
        packed = (blank, blank)
        for i, (ref, k) in enumerate(fields):
            packed = pack(ref, k, b, i, packed)
        send_halo(b, packed)
        wait_halo(b)
        for i, (ref, k) in enumerate(fields):
            unpack(ref, k, b, i)

    def ascend(k, targets):
        w, rate = rates(U, k)
        for j, c in each():
            for point, factor, right_side, index in targets:
                put(U, point, c, j, w[j][c] + factor * STEP * rate[j][c] + at(right_side, index, c, j))

    def coarsest(k):
        w, rate = rates(Fx, k + 4)
        for j, c in each():
            base = at(S, k, c, j) + 16 * STEP * at(R0, k, c, j)
            index = (k + 8) // 4
            g = coarse_rhs(at(G3, index, c, j), at(S, k + 8, c, j), w[j][c] + 8 * STEP * rate[j][c], base)
            if k == 0:
                put(U, 8, c, j, base + g)
                put(U, 5, c, j, w[j][c] + 2 * STEP * rate[j][c] + at(G1, 5, c, j))
                put(U, 6, c, j, w[j][c] + 4 * STEP * rate[j][c] + at(G2, 3, c, j))
            else:
                put(G4, 0, c, j, g)

    def return_points(first):
        def one(d, carry):
            k = first + lax.rem(z + d, 8)
            send_back(0, k)

            @pl.when(k < NT)
            def _():
                send_back(1, k)

            return carry

        lax.fori_loop(0, 8, one, 0)

    def halos_of(first, b, n):
        wait_halo(b)

        def one(i, carry):
            unpack(S, first + i, b, i)
            return carry

        lax.fori_loop(0, n, one, 0)

    halos_of(1, 1, 8)
    descend(0)
    exchange(3, ((Fx, 4), (G3, 2)))
    coarsest(0)
    ascend(6, ((7, 2, G1, 7),))
    return_points(1)

    halos_of(9, 2, 7)
    descend(1)
    exchange(4, ((Fx, 12), (G3, 3)))
    coarsest(8)
    ascend(8, ((9, 2, G1, 9), (10, 4, G2, 5), (12, 8, G3, 3), (16, 16, G4, 0)))
    ascend(10, ((11, 2, G1, 11),))
    ascend(12, ((13, 2, G1, 13), (14, 4, G2, 7)))
    ascend(14, ((15, 2, G1, 15),))
    return_points(9)

    @pl.when(me == 0)
    def _():
        copy = pltpu.make_async_copy(initial, prior.at[:, 8 : 8 + BLOCK_ROWS, :], ret_local.at[1])
        copy.start()
        copy.wait()

    def settle(slot):
        def one(peer, c):
            @pl.when(peer != me)
            def _():
                if slot == 0:
                    dst = out.at[1, :, rows_of(peer), cols_of(peer)]
                else:
                    dst = prior.at[:, prior_rows(peer), cols_of(peer)]
                pltpu.make_async_remote_copy(
                    src_ref=core(U, 1),
                    dst_ref=dst,
                    send_sem=ret_send.at[slot, 1],
                    recv_sem=ret_recv.at[slot, peer],
                    device_id={"tm": peer},
                    device_id_type=MESH,
                ).wait_recv()

            return c

        lax.fori_loop(0, NT, one, 0)
        back(slot, 1)[2].wait()

    @pl.when(me != 0)
    def _():
        settle(1)

    def edge_pack(g, packed):
        last, first = packed
        rows = pl.ds(pl.multiple_of(8 + g * ROWS, 8), ROWS)
        for c in range(2):
            index = 2 * g + c
            tail = prior[c, rows, BLOCK_COLS - 128 : BLOCK_COLS]
            head = prior[c, rows, 0:128]
            last = jnp.where(core_lane == index, pltpu.roll(tail, index + 1, 1), last)
            first = jnp.where(core_lane == index, pltpu.roll(head, index, 1), first)
        return last, first

    packed = lax.fori_loop(0, 8, edge_pack, (blank, blank))
    edge_col_out[0], edge_col_out[1] = packed
    for c in range(2):
        edge_row_out[0, c : c + 1, :] = prior[c, 8 + BLOCK_ROWS - 1 : 8 + BLOCK_ROWS, :]
        edge_row_out[1, c : c + 1, :] = prior[c, 8:9, :]
    edges = [
        pltpu.make_async_remote_copy(
            src_ref=src.at[i],
            dst_ref=dst.at[i],
            send_sem=edge_send.at[n],
            recv_sem=edge_recv.at[n],
            device_id=block_sides[to],
            device_id_type=MESH,
        )
        for n, (to, src, dst, i) in enumerate(
            (
                (0, edge_row_out, edge_row_in, 0),
                (0, edge_row_out, edge_row_in, 1),
                (1, edge_col_out, edge_col_in, 0),
                (2, edge_col_out, edge_col_in, 1),
            )
        )
    ]
    for copy in edges:
        copy.start()
    for copy in edges:
        copy.wait_recv()
    for c in range(2):
        prior[c, 7:8, :] = edge_row_in[0, c : c + 1, :]
        prior[c, 8 + BLOCK_ROWS : 9 + BLOCK_ROWS, :] = edge_row_in[1, c : c + 1, :]

    def final_copy(g):
        rows = pl.ds(pl.multiple_of(g * ROWS, ROWS), ROWS)
        return pltpu.make_async_copy(final.at[:, rows, :], out.at[0, :, rows, :], final_sem.at[g])

    block_tiles = BLOCK_COLS // 128

    def last_step(g, carry):
        around = pl.ds(pl.multiple_of(g * ROWS, ROWS), ROWS + 16)
        rows = pl.ds(pl.multiple_of(g * ROWS, ROWS), ROWS)
        y = [[prior[c, around, lanes(j)] for c in range(2)] for j in range(block_tiles)]
        w = [[y[j][c][8 : 8 + ROWS] for c in range(2)] for j in range(block_tiles)]
        up = [[pltpu.roll(w[j][c], 1, 1) for c in range(2)] for j in range(block_tiles)]
        down = [[pltpu.roll(w[j][c], 127, 1) for c in range(2)] for j in range(block_tiles)]
        before = [pltpu.roll(edge_col_in[0], lax.rem(128 - (2 * g + c), 128), 1) for c in range(2)]
        after = [pltpu.roll(edge_col_in[1], 127 - (2 * g + c), 1) for c in range(2)]
        for j in range(block_tiles):
            west_w, east_w, south_w, north_w = slopes(*w[j])
            for c in range(2):
                x = w[j][c]
                west = pltpu.roll(y[j][c], 1, 0)[8 : 8 + ROWS]
                east = pltpu.roll(y[j][c], ROWS + 15, 0)[8 : 8 + ROWS]
                south = jnp.where(core_lane == 0, up[j - 1][c] if j > 0 else before[c], up[j][c])
                north = jnp.where(core_lane == 127, down[j + 1][c] if j < block_tiles - 1 else after[c], down[j][c])
                rate = (
                    west_w * (west - x)
                    + east_w * (east - x)
                    + south_w * (south - x)
                    + north_w * (north - x)
                    + final[c, rows, lanes(j)]
                )
                final[c, rows, lanes(j)] = x + STEP * rate
        final_copy(g).start()
        return carry

    load = pltpu.make_async_copy(forcing, final, local_sem.at[3])
    load.start()
    load.wait()
    lax.fori_loop(0, 8, last_step, 0)

    for b in range(NB):
        for copy in halo_copies(b):
            copy.wait_send()
    for copy in edges:
        copy.wait_send()

    def finish(peer, c):
        @pl.when(peer != me)
        def _():
            forward(peer).wait_send()
            back(0, peer + 1)[1].wait_send()

            @pl.when(peer > 0)
            def _():
                back(1, peer)[1].wait_send()

        return c

    lax.fori_loop(0, NT, finish, 0)
    settle(0)

    def finish_final(g, c):
        final_copy(g).wait()
        return c

    lax.fori_loop(0, 8, finish_final, 0)


def body(initial, forcing, guess):
    f32 = jnp.float32

    def field(n):
        return pltpu.VMEM((n, 2, HELD_ROWS, HELD_COLS), f32)

    scratch = [field(n) for n in (17, 1, 16, 16, 17, 9, 5, 1, 17, 17)]
    scratch += [
        pltpu.VMEM((2, BLOCK_ROWS + 16, BLOCK_COLS), f32),
        pltpu.VMEM((2, BLOCK_ROWS, BLOCK_COLS), f32),
        pltpu.VMEM((NB, 2, ROWS, 128), f32),
        pltpu.VMEM((NB, 2, ROWS, 128), f32),
        pltpu.VMEM((NB, 2, 2, 8, 128), f32),
        pltpu.VMEM((NB, 2, HELD_ROWS, 128), f32),
        pltpu.VMEM((2, 2, BLOCK_COLS), f32),
        pltpu.VMEM((2, 2, BLOCK_COLS), f32),
        pltpu.VMEM((2, ROWS, 128), f32),
        pltpu.VMEM((2, ROWS, 128), f32),
    ]
    for _ in range(2):
        scratch += [pltpu.VMEM((2, n, 2, HALO, COLS), f32) for n in BATCH]
    dma = pltpu.SemaphoreType.DMA
    scratch += [dma((4,)), dma((NT,)), dma((NT,)), dma((NB, 8)), dma((NB, 8)), dma((2, NT + 1)), dma((2, NT)), dma((2,))]
    scratch += [dma((4,)), dma((4,)), dma((8,))]
    spec = pl.BlockSpec(memory_space=pltpu.HBM)
    return pl.pallas_call(
        kernel,
        out_shape=jax.ShapeDtypeStruct((2, 2, BLOCK_ROWS, BLOCK_COLS), f32),
        in_specs=[spec] * 3,
        out_specs=spec,
        scratch_shapes=scratch,
        compiler_params=pltpu.CompilerParams(
            collective_id=0, has_side_effects=True, vmem_limit_bytes=56 * 1024 * 1024
        ),
        name="cycle",
    )(initial, forcing, guess)


def solution(mesh):
    in_specs = (P(None, "sx", "sy"), P(None, "sx", "sy"), P("tm", None, "sx", "sy"))
    out_specs = P("tm", None, "sx", "sy")
    return jax.shard_map(body, mesh=mesh, in_specs=in_specs, out_specs=out_specs, check_vma=False)
```

time: 577 us -> 112 us (0.19)
  the two profiles are of different devices: /device:TPU:2 before, /device:TPU:82 now
where the time goes in v2:
time: 112 us; the launch traced here: 111 us
  Pallas kernels  108 us (96%)
  local copies, waits for them, and re-layouts  3.08 us (3%)
    pallas_call x1, Pallas kernels, body(): pl.pallas_call(kernel, out_shape=jax.ShapeDtypeStruct((2, 2, BLOCK_ROWS,...  108 us
    unnamed x1, local copies, waits for them, and re-layouts  3.08 us

profile of v2, /device:TPU:82, one launch (start us, length us, event | category | flops | bytes accessed | tf_op | source)
XLA Modules:
  0.0 111.4 jit_solution(1237200548384633332)
XLA Ops:
  0.0 108.4 %cycle.1 = f32[2,2,256,512]{3,2,1,0:T(8,128)} custom-call(f32[2,256,512]{2,1,0:T(8,128)} %initial.1, f32[2,256,512]{2,1,0:T(8,128)} %forcing.1, f32[1,2,256,512]{3,2,1,0:T(8,128)} %guess.1), custom_call_target="tpu_custom_call" | custom-call | tf_op jit(solution)/shard_map/cycle/pallas_call | solution.py:568
  108.4 3.1 %copy.5 = f32[2,2,256,512]{3,2,1,0:T(8,128)} copy(f32[2,2,256,512]{3,2,1,0:T(8,128)} %cycle.1) | data formatting | bytes 4194304

commit v3 on v2

--- a/solution.py
+++ b/solution.py
@@ -25,7 +25,7 @@
     (edge_row_out, edge_row_in, edge_col_out, edge_col_in) = scratch[16:20]
     row_out = scratch[20 : 20 + NB]
     row_in = scratch[20 + NB : 20 + 2 * NB]
-    (local_sem, fwd_send, fwd_recv, halo_send, halo_recv, ret_send, ret_recv, ret_local, edge_send, edge_recv, final_sem) = (
+    (local_sem, fwd_send, fwd_recv, halo_send, halo_recv, ret_send, ret_recv, ret_local, hand_send, edge_send, edge_recv, final_sem) = (
         scratch[20 + 2 * NB :]
     )
 
@@ -116,6 +116,8 @@
         return c
 
     lax.fori_loop(1, NT, start_forward, 0)
+    load = pltpu.make_async_copy(forcing, final, local_sem.at[3])
+    load.start()
 
     lane = lax.broadcasted_iota(jnp.int32, (HELD_ROWS, 128), 1)
     core_lane = lax.broadcasted_iota(jnp.int32, (ROWS, 128), 1)
@@ -224,32 +226,78 @@
     def put(ref, k, c, j, value):
         ref[k, c, :, lanes(j)] = value
 
+    def landing(slot, t):
+        if slot == 0:
+            return out.at[1, :, rows_of(t), cols_of(t)]
+        return prior.at[:, prior_rows(t), cols_of(t)]
+
+    def first_slot(k, t):
+        away = lax.rem(lax.rem(t, 8) - lax.rem(k - 1, 8) + 8, 8)
+        return jnp.where(jnp.logical_and(k < NT, jnp.logical_and(away >= 1, away <= 4)), 1, 0)
+
     def back(slot, k):
-        if slot == 0:
-            dst, to = out.at[1, :, own_rows, own_cols], k - 1
-        else:
-            dst, to = prior.at[:, prior_rows(me), own_cols], k
-        src = core(U, k)
-        remote = pltpu.make_async_remote_copy(
-            src_ref=src,
-            dst_ref=dst,
-            send_sem=ret_send.at[slot, k],
+        return pltpu.make_async_remote_copy(
+            src_ref=core(U, k),
+            dst_ref=landing(slot, me),
+            send_sem=ret_send.at[k],
             recv_sem=ret_recv.at[slot, me],
-            device_id={"tm": to},
+            device_id={"tm": k - 1 + slot},
             device_id_type=MESH,
         )
-        return to, remote, pltpu.make_async_copy(src, dst, ret_local.at[slot])
-
-    def send_back(slot, k):
-        to, remote, local = back(slot, k)
-
-        @pl.when(me == to)
+
+    def own(slot):
+        return pltpu.make_async_copy(core(U, me + 1 - slot), landing(slot, me), ret_local.at[slot])
+
+    def send_back(k):
+        for slot in range(2):
+
+            @pl.when(first_slot(k, me) == slot)
+            def _(slot=slot):
+                @pl.when(me == k - 1 + slot)
+                def _():
+                    own(slot).start()
+
+                @pl.when(me != k - 1 + slot)
+                def _():
+                    back(slot, k).start()
+
+    def hand_on(slot, t):
+        return pltpu.make_async_remote_copy(
+            src_ref=landing(slot, t),
+            dst_ref=landing(1 - slot, t),
+            send_sem=hand_send.at[slot, t],
+            recv_sem=ret_recv.at[1 - slot, t],
+            device_id={"tm": jnp.clip(me + 1 - 2 * slot, 0, NT - 1)},
+            device_id_type=MESH,
+        )
+
+    def wait_landed(slot, t, local):
+        if local:
+
+            @pl.when(t == me)
+            def _():
+                own(slot).wait()
+
+        @pl.when(t != me)
         def _():
-            local.start()
-
-        @pl.when(me != to)
-        def _():
-            remote.start()
+            pltpu.make_async_remote_copy(
+                src_ref=core(U, 1),
+                dst_ref=landing(slot, t),
+                send_sem=ret_send.at[1],
+                recv_sem=ret_recv.at[slot, t],
+                device_id={"tm": t},
+                device_id_type=MESH,
+            ).wait_recv()
+
+    def near(slot, i):
+        step = i // 2
+        along = lax.rem(z + 8 - step, 8) if slot == 0 else lax.rem(z + step, 8)
+        return lax.rem(i, 2) * 8 + along
+
+    def far(slot, i):
+        step = 1 + i // 2
+        along = lax.rem(z + step, 8) if slot == 0 else lax.rem(z + 8 - step, 8)
+        return lax.rem(i, 2) * 8 + along
 
     for copy in stage_in:
         copy.wait()
@@ -337,6 +385,8 @@
         for i, (ref, k) in enumerate(fields):
             packed = pack(ref, k, b, i, packed)
         send_halo(b, packed)
+
+    def exchanged(b, fields):
         wait_halo(b)
         for i, (ref, k) in enumerate(fields):
             unpack(ref, k, b, i)
@@ -363,12 +413,7 @@
     def return_points(first):
         def one(d, carry):
             k = first + lax.rem(z + d, 8)
-            send_back(0, k)
-
-            @pl.when(k < NT)
-            def _():
-                send_back(1, k)
-
+            send_back(k)
             return carry
 
         lax.fori_loop(0, 8, one, 0)
@@ -384,14 +429,17 @@
 
     halos_of(1, 1, 8)
     descend(0)
-    exchange(3, ((Fx, 4), (G3, 2)))
+    fields_a = ((Fx, 4), (G3, 2))
+    fields_b = ((Fx, 12), (G3, 3))
+    exchange(3, fields_a)
+    halos_of(9, 2, 7)
+    descend(1)
+    exchange(4, fields_b)
+    exchanged(3, fields_a)
     coarsest(0)
     ascend(6, ((7, 2, G1, 7),))
     return_points(1)
-
-    halos_of(9, 2, 7)
-    descend(1)
-    exchange(4, ((Fx, 12), (G3, 3)))
+    exchanged(4, fields_b)
     coarsest(8)
     ascend(8, ((9, 2, G1, 9), (10, 4, G2, 5), (12, 8, G3, 3), (16, 16, G4, 0)))
     ascend(10, ((11, 2, G1, 11),))
@@ -399,37 +447,37 @@
     ascend(14, ((15, 2, G1, 15),))
     return_points(9)
 
+    def pass_on(i, carry):
+        @pl.when(me < NT - 1)
+        def _():
+            wait_landed(0, near(0, i), True)
+            hand_on(0, near(0, i)).start()
+
+        @pl.when(me > 0)
+        def _():
+            wait_landed(1, near(1, i), True)
+            hand_on(1, near(1, i)).start()
+
+        return carry
+
+    lax.fori_loop(0, 8, pass_on, 0)
+
     @pl.when(me == 0)
     def _():
         copy = pltpu.make_async_copy(initial, prior.at[:, 8 : 8 + BLOCK_ROWS, :], ret_local.at[1])
         copy.start()
         copy.wait()
 
-    def settle(slot):
-        def one(peer, c):
-            @pl.when(peer != me)
-            def _():
-                if slot == 0:
-                    dst = out.at[1, :, rows_of(peer), cols_of(peer)]
-                else:
-                    dst = prior.at[:, prior_rows(peer), cols_of(peer)]
-                pltpu.make_async_remote_copy(
-                    src_ref=core(U, 1),
-                    dst_ref=dst,
-                    send_sem=ret_send.at[slot, 1],
-                    recv_sem=ret_recv.at[slot, peer],
-                    device_id={"tm": peer},
-                    device_id_type=MESH,
-                ).wait_recv()
-
-            return c
-
-        lax.fori_loop(0, NT, one, 0)
-        back(slot, 1)[2].wait()
-
-    @pl.when(me != 0)
+    def rest(slot):
+        def one(i, carry):
+            wait_landed(slot, far(slot, i), False)
+            return carry
+
+        lax.fori_loop(0, 8, one, 0)
+
+    @pl.when(me > 0)
     def _():
-        settle(1)
+        rest(1)
 
     def edge_pack(g, packed):
         last, first = packed
@@ -507,8 +555,6 @@
         final_copy(g).start()
         return carry
 
-    load = pltpu.make_async_copy(forcing, final, local_sem.at[3])
-    load.start()
     load.wait()
     lax.fori_loop(0, 8, last_step, 0)
 
@@ -518,20 +564,46 @@
     for copy in edges:
         copy.wait_send()
 
-    def finish(peer, c):
-        @pl.when(peer != me)
+    def finish(i, c):
+        @pl.when(i != me)
         def _():
-            forward(peer).wait_send()
-            back(0, peer + 1)[1].wait_send()
-
-            @pl.when(peer > 0)
-            def _():
-                back(1, peer)[1].wait_send()
+            forward(i).wait_send()
+
+        k = i + 1
+        for slot in range(2):
+
+            @pl.when(jnp.logical_and(first_slot(k, me) == slot, me != k - 1 + slot))
+            def _(slot=slot):
+                back(slot, k).wait_send()
 
         return c
 
     lax.fori_loop(0, NT, finish, 0)
-    settle(0)
+
+    def finish_handed(i, c):
+        @pl.when(me < NT - 1)
+        def _():
+            hand_on(0, near(0, i)).wait_send()
+
+        @pl.when(me > 0)
+        def _():
+            hand_on(1, near(1, i)).wait_send()
+
+        return c
+
+    lax.fori_loop(0, 8, finish_handed, 0)
+
+    @pl.when(me < NT - 1)
+    def _():
+        rest(0)
+
+    @pl.when(me == NT - 1)
+    def _():
+        def one(t, c):
+            wait_landed(0, t, True)
+            return c
+
+        lax.fori_loop(0, NT, one, 0)
 
     def finish_final(g, c):
         final_copy(g).wait()
@@ -562,17 +634,17 @@
     for _ in range(2):
         scratch += [pltpu.VMEM((2, n, 2, HALO, COLS), f32) for n in BATCH]
     dma = pltpu.SemaphoreType.DMA
-    scratch += [dma((4,)), dma((NT,)), dma((NT,)), dma((NB, 8)), dma((NB, 8)), dma((2, NT + 1)), dma((2, NT)), dma((2,))]
-    scratch += [dma((4,)), dma((4,)), dma((8,))]
+    scratch += [dma((4,)), dma((NT,)), dma((NT,)), dma((NB, 8)), dma((NB, 8)), dma((NT + 1,)), dma((2, NT)), dma((2,))]
+    scratch += [dma((2, NT)), dma((4,)), dma((4,)), dma((8,))]
     spec = pl.BlockSpec(memory_space=pltpu.HBM)
     return pl.pallas_call(
         kernel,
         out_shape=jax.ShapeDtypeStruct((2, 2, BLOCK_ROWS, BLOCK_COLS), f32),
         in_specs=[spec] * 3,
-        out_specs=spec,
+        out_specs=pl.BlockSpec(memory_space=pl.ANY),
         scratch_shapes=scratch,
         compiler_params=pltpu.CompilerParams(
-            collective_id=0, has_side_effects=True, vmem_limit_bytes=56 * 1024 * 1024
+            collective_id=0, has_side_effects=True, vmem_limit_bytes=32 * 1024 * 1024
         ),
         name="cycle",
     )(initial, forcing, guess)

time: 112 us -> 94.8 us (0.85)
  the two profiles are of different devices: /device:TPU:82 before, /device:TPU:2 now
where the time goes in v3:
time: 94.8 us; the launch traced here: 94.6 us
  Pallas kernels  89.6 us (95%)
  local copies, waits for them, and re-layouts  4.99 us (5%)
    pallas_call x1, Pallas kernels, body(): pl.pallas_call(kernel, out_shape=jax.ShapeDtypeStruct((2, 2, BLOCK_ROWS,...  89.6 us
    unnamed x7, local copies, waits for them, and re-layouts  4.99 us

profile of v3, /device:TPU:2, one launch (start us, length us, event | category | flops | bytes accessed | tf_op | source)
XLA Modules:
  0.0 94.6 jit_solution(14658214606884185205)
XLA Ops:
  0.0 0.0 copy-start
  0.0 1.2 %copy-done = f32[2,256,512]{2,1,0:T(8,128)S(1)} copy-done((f32[2,256,512]{2,1,0:T(8,128)S(1)}, f32[2,256,512]{2,1,0:T(8,128)}, u32[]{:S(2)}) %copy-start) | copy-done | bytes 1048600
  1.2 0.0 copy-start.1
  1.2 1.2 %copy-done.1 = f32[2,256,512]{2,1,0:T(8,128)S(1)} copy-done((f32[2,256,512]{2,1,0:T(8,128)S(1)}, f32[2,256,512]{2,1,0:T(8,128)}, u32[]{:S(2)}) %copy-start.1) | copy-done | bytes 1048600
  2.5 0.0 copy-start.2
  2.5 1.2 %copy-done.2 = f32[1,2,256,512]{3,2,1,0:T(8,128)S(1)} copy-done((f32[1,2,256,512]{3,2,1,0:T(8,128)S(1)}, f32[1,2,256,512]{3,2,1,0:T(8,128)}, u32[]{:S(2)}) %copy-start.2) | copy-done | bytes 1048600
  3.7 89.6 %cycle.1 = f32[2,2,256,512]{3,2,1,0:T(8,128)S(1)} custom-call(f32[2,256,512]{2,1,0:T(8,128)S(1)} %copy-done, f32[2,256,512]{2,1,0:T(8,128)S(1)} %copy-done.1, f32[1,2,256,512]{3,2,1,0:T(8,128)S(1)} %copy-done.2), custom_call_target="tpu_custom_call" | custom-call | tf_op jit(solution)/shard_map/cycle/pallas_call | solution.py:640
  93.3 1.3 %copy.5 = f32[2,2,256,512]{3,2,1,0:T(8,128)} copy(f32[2,2,256,512]{3,2,1,0:T(8,128)S(1)} %cycle.1) | data formatting | bytes 4194304
Async XLA Ops:
  0.0 1.2 %copy-start = (f32[2,256,512]{2,1,0:T(8,128)S(1)}, f32[2,256,512]{2,1,0:T(8,128)}, u32[]{:S(2)}) copy-start(f32[2,256,512]{2,1,0:T(8,128)} %initial.1) | copy-start | bytes 3145732
  1.2 1.2 %copy-start.1 = (f32[2,256,512]{2,1,0:T(8,128)S(1)}, f32[2,256,512]{2,1,0:T(8,128)}, u32[]{:S(2)}) copy-start(f32[2,256,512]{2,1,0:T(8,128)} %forcing.1) | copy-start | bytes 3145732
  2.5 1.2 %copy-start.2 = (f32[1,2,256,512]{3,2,1,0:T(8,128)S(1)}, f32[1,2,256,512]{3,2,1,0:T(8,128)}, u32[]{:S(2)}) copy-start(f32[1,2,256,512]{3,2,1,0:T(8,128)} %guess.1) | copy-start | bytes 3145732

commit v4 on v3

--- a/solution.py
+++ b/solution.py
@@ -21,11 +21,11 @@
 
 
 def kernel(initial, forcing, guess, out, *scratch):
-    (S, F, R0, T1, G1, G2, G3, G4, Fx, U, prior, final, col_out, col_in, corner_in, wide) = scratch[:16]
+    (S, F, R0, T1, G1, G2, G3, G4, Fx, U, prior, block_forcing, col_out, col_in, corner_in, wide) = scratch[:16]
     (edge_row_out, edge_row_in, edge_col_out, edge_col_in) = scratch[16:20]
     row_out = scratch[20 : 20 + NB]
     row_in = scratch[20 + NB : 20 + 2 * NB]
-    (local_sem, fwd_send, fwd_recv, halo_send, halo_recv, ret_send, ret_recv, ret_local, hand_send, edge_send, edge_recv, final_sem) = (
+    (local_sem, fwd_send, fwd_recv, halo_send, halo_recv, ret_send, ret_recv, ret_local, hand_send, edge_send, edge_recv) = (
         scratch[20 + 2 * NB :]
     )
 
@@ -116,7 +116,7 @@
         return c
 
     lax.fori_loop(1, NT, start_forward, 0)
-    load = pltpu.make_async_copy(forcing, final, local_sem.at[3])
+    load = pltpu.make_async_copy(forcing, block_forcing, local_sem.at[3])
     load.start()
 
     lane = lax.broadcasted_iota(jnp.int32, (HELD_ROWS, 128), 1)
@@ -335,10 +335,9 @@
         residual = g - (point - image)
         return residual + point - base
 
-    def descend(half):
-        start = 8 * half
-
-        def fine(k, carry):
+    def descend(q):
+        def fine(i, carry):
+            k = 4 * q + i
             w, rate = rates(S, k)
             for j, c in each():
                 put(R0, k, c, j, rate[j][c])
@@ -351,9 +350,10 @@
                 put(Fx, k + 1, c, j, base + g)
             return carry
 
-        lax.fori_loop(start, start + 8, fine, 0)
-
-        def second(m, carry):
+        lax.fori_loop(0, 4, fine, 0)
+
+        def second(i, carry):
+            m = 2 * q + i
             k = 2 * m
             w, rate = rates(Fx, k + 1)
             for j, c in each():
@@ -363,22 +363,19 @@
                 put(Fx, k + 2, c, j, base + g)
             return carry
 
-        lax.fori_loop(start // 2, start // 2 + 4, second, 0)
-
-        for q in (2 * half, 2 * half + 1):
-            k = 4 * q
-            w, rate = rates(Fx, k + 2)
-            for j, c in each():
-                base = at(S, k, c, j) + 8 * STEP * at(R0, k, c, j)
-                g = coarse_rhs(at(G2, 2 * q + 2, c, j), at(S, k + 4, c, j), w[j][c] + 4 * STEP * rate[j][c], base)
-                put(G3, q + 1, c, j, g)
-                if q % 2 == 0:
-                    put(Fx, k + 4, c, j, base + g)
-                if q == 0:
-                    put(U, 1, c, j, at(Fx, 1, c, j))
-                    put(U, 2, c, j, w[j][c])
-                    put(U, 3, c, j, w[j][c] + 2 * STEP * rate[j][c] + at(G1, 3, c, j))
-                    put(U, 4, c, j, base + g)
+        lax.fori_loop(0, 2, second, 0)
+
+        k = 4 * q
+        w, rate = rates(Fx, k + 2)
+        for j, c in each():
+            base = at(S, k, c, j) + 8 * STEP * at(R0, k, c, j)
+            g = coarse_rhs(at(G2, 2 * q + 2, c, j), at(S, k + 4, c, j), w[j][c] + 4 * STEP * rate[j][c], base)
+            put(G3, q + 1, c, j, g)
+            put(Fx, k + 4, c, j, base + g)
+            put(U, k + 1, c, j, at(Fx, k + 1, c, j))
+            put(U, k + 2, c, j, w[j][c])
+            put(U, k + 3, c, j, w[j][c] + 2 * STEP * rate[j][c] + at(G1, k + 3, c, j))
+            put(U, k + 4, c, j, base + g)
 
     def exchange(b, fields):
         packed = (blank, blank)
@@ -410,13 +407,12 @@
             else:
                 put(G4, 0, c, j, g)
 
-    def return_points(first):
+    def return_points(first, n):
         def one(d, carry):
-            k = first + lax.rem(z + d, 8)
-            send_back(k)
+            send_back(first + lax.rem(z + d, n))
             return carry
 
-        lax.fori_loop(0, 8, one, 0)
+        lax.fori_loop(0, n, one, 0)
 
     def halos_of(first, b, n):
         wait_halo(b)
@@ -429,23 +425,25 @@
 
     halos_of(1, 1, 8)
     descend(0)
+    descend(1)
     fields_a = ((Fx, 4), (G3, 2))
     fields_b = ((Fx, 12), (G3, 3))
     exchange(3, fields_a)
     halos_of(9, 2, 7)
-    descend(1)
+    descend(2)
+    descend(3)
     exchange(4, fields_b)
     exchanged(3, fields_a)
     coarsest(0)
     ascend(6, ((7, 2, G1, 7),))
-    return_points(1)
+    return_points(1, 8)
     exchanged(4, fields_b)
     coarsest(8)
     ascend(8, ((9, 2, G1, 9), (10, 4, G2, 5), (12, 8, G3, 3), (16, 16, G4, 0)))
     ascend(10, ((11, 2, G1, 11),))
     ascend(12, ((13, 2, G1, 13), (14, 4, G2, 7)))
     ascend(14, ((15, 2, G1, 15),))
-    return_points(9)
+    return_points(9, 8)
 
     def pass_on(i, carry):
         @pl.when(me < NT - 1)
@@ -520,10 +518,6 @@
     for c in range(2):
         prior[c, 7:8, :] = edge_row_in[0, c : c + 1, :]
         prior[c, 8 + BLOCK_ROWS : 9 + BLOCK_ROWS, :] = edge_row_in[1, c : c + 1, :]
-
-    def final_copy(g):
-        rows = pl.ds(pl.multiple_of(g * ROWS, ROWS), ROWS)
-        return pltpu.make_async_copy(final.at[:, rows, :], out.at[0, :, rows, :], final_sem.at[g])
 
     block_tiles = BLOCK_COLS // 128
 
@@ -549,10 +543,9 @@
                     + east_w * (east - x)
                     + south_w * (south - x)
                     + north_w * (north - x)
-                    + final[c, rows, lanes(j)]
+                    + block_forcing[c, rows, lanes(j)]
                 )
-                final[c, rows, lanes(j)] = x + STEP * rate
-        final_copy(g).start()
+                out[0, c, rows, lanes(j)] = x + STEP * rate
         return carry
 
     load.wait()
@@ -604,12 +597,6 @@
             return c
 
         lax.fori_loop(0, NT, one, 0)
-
-    def finish_final(g, c):
-        final_copy(g).wait()
-        return c
-
-    lax.fori_loop(0, 8, finish_final, 0)
 
 
 def body(initial, forcing, guess):
@@ -635,19 +622,19 @@
         scratch += [pltpu.VMEM((2, n, 2, HALO, COLS), f32) for n in BATCH]
     dma = pltpu.SemaphoreType.DMA
     scratch += [dma((4,)), dma((NT,)), dma((NT,)), dma((NB, 8)), dma((NB, 8)), dma((NT + 1,)), dma((2, NT)), dma((2,))]
-    scratch += [dma((2, NT)), dma((4,)), dma((4,)), dma((8,))]
+    scratch += [dma((2, NT)), dma((4,)), dma((4,))]
     spec = pl.BlockSpec(memory_space=pltpu.HBM)
     return pl.pallas_call(
         kernel,
-        out_shape=jax.ShapeDtypeStruct((2, 2, BLOCK_ROWS, BLOCK_COLS), f32),
+        out_shape=pltpu.VMEM((2, 2, BLOCK_ROWS, BLOCK_COLS), f32),
         in_specs=[spec] * 3,
-        out_specs=pl.BlockSpec(memory_space=pl.ANY),
+        out_specs=pl.BlockSpec(memory_space=pltpu.VMEM),
         scratch_shapes=scratch,
         compiler_params=pltpu.CompilerParams(
             collective_id=0, has_side_effects=True, vmem_limit_bytes=32 * 1024 * 1024
         ),
         name="cycle",
-    )(initial, forcing, guess)
+    )(*(pltpu.with_memory_space_constraint(x, pltpu.HBM) for x in (initial, forcing, guess)))
 
 
 def solution(mesh):

time: 94.8 us -> 90.7 us (0.957)
  local copies, waits for them, and re-layouts: 4.99 us -> 1.32 us
    unnamed x7 -> x1, local copies, waits for them, and re-layouts: 4.99 us -> 1.32 us
where the time goes in v4:
time: 90.7 us; the launch traced here: 90.5 us
  Pallas kernels  89.2 us (98%)
  local copies, waits for them, and re-layouts  1.32 us (1%)
    pallas_call x1, Pallas kernels, body(): pl.pallas_call(kernel, out_shape=pltpu.VMEM((2, 2, BLOCK_ROWS, BLOCK_COLS...  89.2 us

profile of v4, /device:TPU:2, one launch (start us, length us, event | category | flops | bytes accessed | tf_op | source)
XLA Modules:
  0.0 90.5 jit_solution(6712042443842092320)
XLA Ops:
  0.0 89.2 %cycle.1 = f32[2,2,256,512]{3,2,1,0:T(8,128)S(1)} custom-call(f32[2,256,512]{2,1,0:T(8,128)} %initial.1, f32[2,256,512]{2,1,0:T(8,128)} %forcing.1, f32[1,2,256,512]{3,2,1,0:T(8,128)} %guess.1), custom_call_target="tpu_custom_call" | custom-call | tf_op jit(solution)/shard_map/cycle/pallas_call | solution.py:627
  89.2 1.3 %copy.5 = f32[2,2,256,512]{3,2,1,0:T(8,128)} copy(f32[2,2,256,512]{3,2,1,0:T(8,128)S(1)} %cycle.1) | data formatting | bytes 4194304

commit v5 on v4

--- a/solution.py
+++ b/solution.py
@@ -22,11 +22,10 @@
 
 def kernel(initial, forcing, guess, out, *scratch):
     (S, F, R0, T1, G1, G2, G3, G4, Fx, U, prior, block_forcing, col_out, col_in, corner_in, wide) = scratch[:16]
-    (edge_row_out, edge_row_in, edge_col_out, edge_col_in) = scratch[16:20]
-    row_out = scratch[20 : 20 + NB]
-    row_in = scratch[20 + NB : 20 + 2 * NB]
-    (local_sem, fwd_send, fwd_recv, halo_send, halo_recv, ret_send, ret_recv, ret_local, hand_send, edge_send, edge_recv) = (
-        scratch[20 + 2 * NB :]
+    row_out = scratch[16 : 16 + NB]
+    row_in = scratch[16 + NB : 16 + 2 * NB]
+    (local_sem, fwd_send, fwd_recv, halo_send, halo_recv, ret_send, ret_recv, ret_local, hand_send, edge_send, edge_recv, end_send, end_recv) = (
+        scratch[16 + 2 * NB :]
     )
 
     me = lax.axis_index("tm")
@@ -69,6 +68,9 @@
     def prior_rows(t):
         return pl.ds(pl.multiple_of(8 + mirrored(lax.rem(t, 8)) * ROWS, 8), ROWS)
 
+    def prior_cols(t):
+        return pl.ds(pl.multiple_of(128 + (t // 8) * COLS, 128), COLS)
+
     def core(ref, k):
         return ref.at[k, :, 0:ROWS, 0:COLS]
 
@@ -115,7 +117,21 @@
         forward(lax.rem(me + d, NT)).start()
         return c
 
-    lax.fori_loop(1, NT, start_forward, 0)
+    forward(lax.rem(xl + 1, 2) * 8 + lax.rem(z + 4, 8)).start()
+    forward(lax.rem(xl + 0, 2) * 8 + lax.rem(z + 4, 8)).start()
+    forward(lax.rem(xl + 1, 2) * 8 + lax.rem(z + 1, 8)).start()
+    forward(lax.rem(xl + 1, 2) * 8 + lax.rem(z + 7, 8)).start()
+    forward(lax.rem(xl + 1, 2) * 8 + lax.rem(z + 3, 8)).start()
+    forward(lax.rem(xl + 1, 2) * 8 + lax.rem(z + 5, 8)).start()
+    forward(lax.rem(xl + 0, 2) * 8 + lax.rem(z + 1, 8)).start()
+    forward(lax.rem(xl + 0, 2) * 8 + lax.rem(z + 7, 8)).start()
+    forward(lax.rem(xl + 0, 2) * 8 + lax.rem(z + 3, 8)).start()
+    forward(lax.rem(xl + 0, 2) * 8 + lax.rem(z + 5, 8)).start()
+    forward(lax.rem(xl + 1, 2) * 8 + lax.rem(z + 2, 8)).start()
+    forward(lax.rem(xl + 1, 2) * 8 + lax.rem(z + 6, 8)).start()
+    forward(lax.rem(xl + 0, 2) * 8 + lax.rem(z + 2, 8)).start()
+    forward(lax.rem(xl + 0, 2) * 8 + lax.rem(z + 6, 8)).start()
+    forward(lax.rem(xl + 1, 2) * 8 + lax.rem(z + 0, 8)).start()
     load = pltpu.make_async_copy(forcing, block_forcing, local_sem.at[3])
     load.start()
 
@@ -229,7 +245,7 @@
     def landing(slot, t):
         if slot == 0:
             return out.at[1, :, rows_of(t), cols_of(t)]
-        return prior.at[:, prior_rows(t), cols_of(t)]
+        return prior.at[:, prior_rows(t), prior_cols(t)]
 
     def first_slot(k, t):
         away = lax.rem(lax.rem(t, 8) - lax.rem(k - 1, 8) + 8, 8)
@@ -407,12 +423,9 @@
             else:
                 put(G4, 0, c, j, g)
 
-    def return_points(first, n):
-        def one(d, carry):
-            send_back(first + lax.rem(z + d, n))
-            return carry
-
-        lax.fori_loop(0, n, one, 0)
+    def return_points(first, offsets=(3, -4, 0, -1, 2, -3, 1, -2)):
+        for offset in offsets:
+            send_back(first + lax.rem(z + offset + 8, 8))
 
     def halos_of(first, b, n):
         wait_halo(b)
@@ -423,27 +436,70 @@
 
         lax.fori_loop(0, n, one, 0)
 
+    fields_a = ((Fx, 4), (G3, 2))
+    fields_b = ((Fx, 12), (G3, 3))
     halos_of(1, 1, 8)
     descend(0)
     descend(1)
-    fields_a = ((Fx, 4), (G3, 2))
-    fields_b = ((Fx, 12), (G3, 3))
     exchange(3, fields_a)
     halos_of(9, 2, 7)
     descend(2)
-    descend(3)
     exchange(4, fields_b)
     exchanged(3, fields_a)
     coarsest(0)
     ascend(6, ((7, 2, G1, 7),))
-    return_points(1, 8)
+    return_points(1)
+    descend(3)
     exchanged(4, fields_b)
     coarsest(8)
     ascend(8, ((9, 2, G1, 9), (10, 4, G2, 5), (12, 8, G3, 3), (16, 16, G4, 0)))
     ascend(10, ((11, 2, G1, 11),))
     ascend(12, ((13, 2, G1, 13), (14, 4, G2, 7)))
     ascend(14, ((15, 2, G1, 15),))
-    return_points(9, 8)
+    return_points(9)
+
+    def side_edge(t):
+        first = t // 8 == 0
+        return pltpu.make_async_remote_copy(
+            src_ref=prior.at[:, prior_rows(t), pl.ds(pl.multiple_of(jnp.where(first, 128, BLOCK_COLS), 128), 128)],
+            dst_ref=prior.at[:, prior_rows(t), pl.ds(pl.multiple_of(jnp.where(first, 128 + BLOCK_COLS, 0), 128), 128)],
+            send_sem=edge_send.at[t],
+            recv_sem=edge_recv.at[t],
+            device_id={"sy": lax.rem(sy + jnp.where(first, 7, 1), 8)},
+            device_id_type=MESH,
+        )
+
+    def end_edge(t, last):
+        src, dst = (BLOCK_ROWS, 0) if last else (8, 8 + BLOCK_ROWS)
+        return pltpu.make_async_remote_copy(
+            src_ref=prior.at[:, src : src + 8, prior_cols(t)],
+            dst_ref=prior.at[:, dst : dst + 8, prior_cols(t)],
+            send_sem=end_send.at[2 * (t // 8) + last],
+            recv_sem=end_recv.at[2 * (t // 8) + last],
+            device_id=block_sides[0],
+            device_id_type=MESH,
+        )
+
+    def send_edges(t):
+        side_edge(t).start()
+        for last in range(2):
+
+            @pl.when(mirrored(lax.rem(t, 8)) == 7 * last)
+            def _(last=last):
+                end_edge(t, last).start()
+
+    @pl.when(me == 0)
+    def _():
+        def one(t, carry):
+            send_edges(t)
+            return carry
+
+        copy = pltpu.make_async_copy(
+            initial, prior.at[:, 8 : 8 + BLOCK_ROWS, 128 : 128 + BLOCK_COLS], ret_local.at[1]
+        )
+        copy.start()
+        copy.wait()
+        lax.fori_loop(0, NT, one, 0)
 
     def pass_on(i, carry):
         @pl.when(me < NT - 1)
@@ -455,20 +511,17 @@
         def _():
             wait_landed(1, near(1, i), True)
             hand_on(1, near(1, i)).start()
+            send_edges(near(1, i))
 
         return carry
 
     lax.fori_loop(0, 8, pass_on, 0)
-
-    @pl.when(me == 0)
-    def _():
-        copy = pltpu.make_async_copy(initial, prior.at[:, 8 : 8 + BLOCK_ROWS, :], ret_local.at[1])
-        copy.start()
-        copy.wait()
 
     def rest(slot):
         def one(i, carry):
             wait_landed(slot, far(slot, i), False)
+            if slot == 1:
+                send_edges(far(slot, i))
             return carry
 
         lax.fori_loop(0, 8, one, 0)
@@ -477,59 +530,29 @@
     def _():
         rest(1)
 
-    def edge_pack(g, packed):
-        last, first = packed
-        rows = pl.ds(pl.multiple_of(8 + g * ROWS, 8), ROWS)
-        for c in range(2):
-            index = 2 * g + c
-            tail = prior[c, rows, BLOCK_COLS - 128 : BLOCK_COLS]
-            head = prior[c, rows, 0:128]
-            last = jnp.where(core_lane == index, pltpu.roll(tail, index + 1, 1), last)
-            first = jnp.where(core_lane == index, pltpu.roll(head, index, 1), first)
-        return last, first
-
-    packed = lax.fori_loop(0, 8, edge_pack, (blank, blank))
-    edge_col_out[0], edge_col_out[1] = packed
-    for c in range(2):
-        edge_row_out[0, c : c + 1, :] = prior[c, 8 + BLOCK_ROWS - 1 : 8 + BLOCK_ROWS, :]
-        edge_row_out[1, c : c + 1, :] = prior[c, 8:9, :]
-    edges = [
-        pltpu.make_async_remote_copy(
-            src_ref=src.at[i],
-            dst_ref=dst.at[i],
-            send_sem=edge_send.at[n],
-            recv_sem=edge_recv.at[n],
-            device_id=block_sides[to],
-            device_id_type=MESH,
-        )
-        for n, (to, src, dst, i) in enumerate(
-            (
-                (0, edge_row_out, edge_row_in, 0),
-                (0, edge_row_out, edge_row_in, 1),
-                (1, edge_col_out, edge_col_in, 0),
-                (2, edge_col_out, edge_col_in, 1),
-            )
-        )
-    ]
-    for copy in edges:
-        copy.start()
-    for copy in edges:
-        copy.wait_recv()
-    for c in range(2):
-        prior[c, 7:8, :] = edge_row_in[0, c : c + 1, :]
-        prior[c, 8 + BLOCK_ROWS : 9 + BLOCK_ROWS, :] = edge_row_in[1, c : c + 1, :]
-
     block_tiles = BLOCK_COLS // 128
 
-    def last_step(g, carry):
+    def last_step(i, carry):
+        along = lax.rem(z + jnp.where(i < 4, i, 11 - i), 8)
+        g = mirrored(along)
+        side_edge(along).wait_recv()
+        side_edge(8 + along).wait_recv()
+        for last in range(2):
+
+            @pl.when(g == 7 - 7 * last)
+            def _(last=last):
+                end_edge(0, last).wait_recv()
+                end_edge(8, last).wait_recv()
+
         around = pl.ds(pl.multiple_of(g * ROWS, ROWS), ROWS + 16)
         rows = pl.ds(pl.multiple_of(g * ROWS, ROWS), ROWS)
-        y = [[prior[c, around, lanes(j)] for c in range(2)] for j in range(block_tiles)]
+        inner = pl.ds(pl.multiple_of(8 + g * ROWS, 8), ROWS)
+        y = [[prior[c, around, lanes(j + 1)] for c in range(2)] for j in range(block_tiles)]
         w = [[y[j][c][8 : 8 + ROWS] for c in range(2)] for j in range(block_tiles)]
         up = [[pltpu.roll(w[j][c], 1, 1) for c in range(2)] for j in range(block_tiles)]
         down = [[pltpu.roll(w[j][c], 127, 1) for c in range(2)] for j in range(block_tiles)]
-        before = [pltpu.roll(edge_col_in[0], lax.rem(128 - (2 * g + c), 128), 1) for c in range(2)]
-        after = [pltpu.roll(edge_col_in[1], 127 - (2 * g + c), 1) for c in range(2)]
+        before = [pltpu.roll(prior[c, inner, lanes(0)], 1, 1) for c in range(2)]
+        after = [pltpu.roll(prior[c, inner, lanes(block_tiles + 1)], 127, 1) for c in range(2)]
         for j in range(block_tiles):
             west_w, east_w, south_w, north_w = slopes(*w[j])
             for c in range(2):
@@ -554,8 +577,14 @@
     for b in range(NB):
         for copy in halo_copies(b):
             copy.wait_send()
-    for copy in edges:
-        copy.wait_send()
+    def finish_edges(t, c):
+        side_edge(t).wait_send()
+        return c
+
+    lax.fori_loop(0, NT, finish_edges, 0)
+    for t in (0, 8):
+        for last in range(2):
+            end_edge(t, last).wait_send()
 
     def finish(i, c):
         @pl.when(i != me)
@@ -607,22 +636,18 @@
 
     scratch = [field(n) for n in (17, 1, 16, 16, 17, 9, 5, 1, 17, 17)]
     scratch += [
-        pltpu.VMEM((2, BLOCK_ROWS + 16, BLOCK_COLS), f32),
+        pltpu.VMEM((2, BLOCK_ROWS + 16, BLOCK_COLS + 256), f32),
         pltpu.VMEM((2, BLOCK_ROWS, BLOCK_COLS), f32),
         pltpu.VMEM((NB, 2, ROWS, 128), f32),
         pltpu.VMEM((NB, 2, ROWS, 128), f32),
         pltpu.VMEM((NB, 2, 2, 8, 128), f32),
         pltpu.VMEM((NB, 2, HELD_ROWS, 128), f32),
-        pltpu.VMEM((2, 2, BLOCK_COLS), f32),
-        pltpu.VMEM((2, 2, BLOCK_COLS), f32),
-        pltpu.VMEM((2, ROWS, 128), f32),
-        pltpu.VMEM((2, ROWS, 128), f32),
     ]
     for _ in range(2):
         scratch += [pltpu.VMEM((2, n, 2, HALO, COLS), f32) for n in BATCH]
     dma = pltpu.SemaphoreType.DMA
     scratch += [dma((4,)), dma((NT,)), dma((NT,)), dma((NB, 8)), dma((NB, 8)), dma((NT + 1,)), dma((2, NT)), dma((2,))]
-    scratch += [dma((2, NT)), dma((4,)), dma((4,))]
+    scratch += [dma((2, NT)), dma((NT,)), dma((NT,)), dma((4,)), dma((4,))]
     spec = pl.BlockSpec(memory_space=pltpu.HBM)
     return pl.pallas_call(
         kernel,

time: 90.7 us -> 86.1 us (0.949)
  Pallas kernels: 89.2 us -> 84 us
    pallas_call x1, Pallas kernels: 89.2 us -> 84 us  [body(): pl.pallas_call(kernel, out_shape=pltpu.VMEM((2, 2, BLOCK_ROWS, BLOCK_COLS...]
where the time goes in v5:
time: 86.1 us; the launch traced here: 85.4 us
  Pallas kernels  84 us (98%)
  local copies, waits for them, and re-layouts  1.32 us (2%)
    pallas_call x1, Pallas kernels, body(): pl.pallas_call(kernel, out_shape=pltpu.VMEM((2, 2, BLOCK_ROWS, BLOCK_COLS...  84 us

profile of v5, /device:TPU:2, one launch (start us, length us, event | category | flops | bytes accessed | tf_op | source)
XLA Modules:
  0.0 85.4 jit_solution(11677874382066613093)
XLA Ops:
  0.0 84.0 %cycle.1 = f32[2,2,256,512]{3,2,1,0:T(8,128)S(1)} custom-call(f32[2,256,512]{2,1,0:T(8,128)} %initial.1, f32[2,256,512]{2,1,0:T(8,128)} %forcing.1, f32[1,2,256,512]{3,2,1,0:T(8,128)} %guess.1), custom_call_target="tpu_custom_call" | custom-call | tf_op jit(solution)/shard_map/cycle/pallas_call | solution.py:652
  84.0 1.3 %copy.5 = f32[2,2,256,512]{3,2,1,0:T(8,128)} copy(f32[2,2,256,512]{3,2,1,0:T(8,128)S(1)} %cycle.1) | data formatting | bytes 4194304

commit v6 on v5

--- a/solution.py
+++ b/solution.py
@@ -15,7 +15,7 @@
 HELD_ROWS, HELD_COLS = ROWS + 2 * HALO, COLS + 128
 TILES = HELD_COLS // 128
 STEP = COURANT / (NT * (2.0 + 4.0 * VISCOSITY))
-BATCH = (2, 8, 7, 2, 2)
+BATCH = (2, 4, 4, 7, 2, 2)
 NB = len(BATCH)
 UP, DOWN, RIGHT, LEFT, UP_RIGHT, DOWN_RIGHT, UP_LEFT, DOWN_LEFT = range(8)
 
@@ -320,6 +320,8 @@
     packed = pack(S, 0, 0, 0, (blank, blank))
     send_halo(0, pack(F, 0, 0, 1, packed))
 
+    arrivals = ((1, 1, 4), (5, 2, 4), (9, 3, 7))
+
     def arrive(first, b):
         def one(i, packed):
             k = first + i
@@ -332,8 +334,8 @@
 
         return one
 
-    send_halo(1, lax.fori_loop(0, 8, arrive(1, 1), (blank, blank)))
-    send_halo(2, lax.fori_loop(0, 7, arrive(9, 2), (blank, blank)))
+    for first, b, n in arrivals:
+        send_halo(b, lax.fori_loop(0, n, arrive(first, b), (blank, blank)))
 
     @pl.when(me != NT - 1)
     def _():
@@ -352,8 +354,7 @@
         return residual + point - base
 
     def descend(q):
-        def fine(i, carry):
-            k = 4 * q + i
+        def fine(k, relaxes):
             w, rate = rates(S, k)
             for j, c in each():
                 put(R0, k, c, j, rate[j][c])
@@ -363,10 +364,15 @@
                 base = at(S, k, c, j) + 2 * STEP * at(R0, k, c, j)
                 g = coarse_rhs(0.0, at(S, k + 1, c, j), w[j][c] + STEP * rate[j][c], base)
                 put(G1, k + 1, c, j, g)
-                put(Fx, k + 1, c, j, base + g)
+                if relaxes:
+                    put(Fx, k + 1, c, j, base + g)
+
+        def fine_pair(i, carry):
+            fine(4 * q + 2 * i, True)
+            fine(4 * q + 2 * i + 1, False)
             return carry
 
-        lax.fori_loop(0, 4, fine, 0)
+        lax.fori_loop(0, 2, fine_pair, 0)
 
         def second(i, carry):
             m = 2 * q + i
@@ -388,6 +394,8 @@
             g = coarse_rhs(at(G2, 2 * q + 2, c, j), at(S, k + 4, c, j), w[j][c] + 4 * STEP * rate[j][c], base)
             put(G3, q + 1, c, j, g)
             put(Fx, k + 4, c, j, base + g)
+            if q > 0:
+                continue
             put(U, k + 1, c, j, at(Fx, k + 1, c, j))
             put(U, k + 2, c, j, w[j][c])
             put(U, k + 3, c, j, w[j][c] + 2 * STEP * rate[j][c] + at(G1, k + 3, c, j))
@@ -438,19 +446,20 @@
 
     fields_a = ((Fx, 4), (G3, 2))
     fields_b = ((Fx, 12), (G3, 3))
-    halos_of(1, 1, 8)
+    halos_of(*arrivals[0])
     descend(0)
+    halos_of(*arrivals[1])
     descend(1)
-    exchange(3, fields_a)
-    halos_of(9, 2, 7)
+    exchange(4, fields_a)
+    halos_of(*arrivals[2])
     descend(2)
-    exchange(4, fields_b)
-    exchanged(3, fields_a)
+    exchange(5, fields_b)
+    exchanged(4, fields_a)
     coarsest(0)
     ascend(6, ((7, 2, G1, 7),))
     return_points(1)
     descend(3)
-    exchanged(4, fields_b)
+    exchanged(5, fields_b)
     coarsest(8)
     ascend(8, ((9, 2, G1, 9), (10, 4, G2, 5), (12, 8, G3, 3), (16, 16, G4, 0)))
     ascend(10, ((11, 2, G1, 11),))

time: 86.1 us -> 85.3 us (level)
  no operation moved by 1% of the time
where the time goes in v6:
time: 85.3 us; the launch traced here: 84.6 us
  Pallas kernels  83.3 us (98%)
  local copies, waits for them, and re-layouts  1.32 us (2%)
    pallas_call x1, Pallas kernels, body(): pl.pallas_call(kernel, out_shape=pltpu.VMEM((2, 2, BLOCK_ROWS, BLOCK_COLS...  83.3 us

profile of v6, /device:TPU:2, one launch (start us, length us, event | category | flops | bytes accessed | tf_op | source)
XLA Modules:
  0.0 84.6 jit_solution(16328793888688462292)
XLA Ops:
  0.0 83.3 %cycle.1 = f32[2,2,256,512]{3,2,1,0:T(8,128)S(1)} custom-call(f32[2,256,512]{2,1,0:T(8,128)} %initial.1, f32[2,256,512]{2,1,0:T(8,128)} %forcing.1, f32[1,2,256,512]{3,2,1,0:T(8,128)} %guess.1), custom_call_target="tpu_custom_call" | custom-call | tf_op jit(solution)/shard_map/cycle/pallas_call | solution.py:661
  83.3 1.3 %copy.5 = f32[2,2,256,512]{3,2,1,0:T(8,128)} copy(f32[2,2,256,512]{3,2,1,0:T(8,128)S(1)} %cycle.1) | data formatting | bytes 4194304

commit v7 on v6

--- a/solution.py
+++ b/solution.py
@@ -233,8 +233,8 @@
             result.append(pair)
         return w, result
 
-    def each():
-        return [(j, c) for j in range(TILES) for c in range(2)]
+    def each(halo=True):
+        return [(j, c) for j in range(TILES if halo else TILES - 1) for c in range(2)]
 
     def at(ref, k, c, j):
         return ref[k, c, :, lanes(j)]
@@ -353,26 +353,28 @@
         residual = g - (point - image)
         return residual + point - base
 
+    def fine(k, relaxes):
+        w, rate = rates(S, k)
+        for j, c in each():
+            put(R0, k, c, j, rate[j][c])
+            put(T1, k, c, j, w[j][c] + STEP * rate[j][c])
+        w, rate = rates(T1, k)
+        for j, c in each():
+            base = at(S, k, c, j) + 2 * STEP * at(R0, k, c, j)
+            g = coarse_rhs(0.0, at(S, k + 1, c, j), w[j][c] + STEP * rate[j][c], base)
+            put(G1, k + 1, c, j, g)
+            if relaxes:
+                put(Fx, k + 1, c, j, base + g)
+
     def descend(q):
-        def fine(k, relaxes):
-            w, rate = rates(S, k)
-            for j, c in each():
-                put(R0, k, c, j, rate[j][c])
-                put(T1, k, c, j, w[j][c] + STEP * rate[j][c])
-            w, rate = rates(T1, k)
-            for j, c in each():
-                base = at(S, k, c, j) + 2 * STEP * at(R0, k, c, j)
-                g = coarse_rhs(0.0, at(S, k + 1, c, j), w[j][c] + STEP * rate[j][c], base)
-                put(G1, k + 1, c, j, g)
-                if relaxes:
-                    put(Fx, k + 1, c, j, base + g)
-
         def fine_pair(i, carry):
             fine(4 * q + 2 * i, True)
             fine(4 * q + 2 * i + 1, False)
             return carry
 
-        lax.fori_loop(0, 2, fine_pair, 0)
+        if q == 0:
+            fine(1, False)
+        lax.fori_loop(0 if q > 0 else 1, 2, fine_pair, 0)
 
         def second(i, carry):
             m = 2 * q + i
@@ -389,7 +391,7 @@
 
         k = 4 * q
         w, rate = rates(Fx, k + 2)
-        for j, c in each():
+        for j, c in each(halo=False):
             base = at(S, k, c, j) + 8 * STEP * at(R0, k, c, j)
             g = coarse_rhs(at(G2, 2 * q + 2, c, j), at(S, k + 4, c, j), w[j][c] + 4 * STEP * rate[j][c], base)
             put(G3, q + 1, c, j, g)
@@ -412,15 +414,15 @@
         for i, (ref, k) in enumerate(fields):
             unpack(ref, k, b, i)
 
-    def ascend(k, targets):
+    def ascend(k, targets, halo=True):
         w, rate = rates(U, k)
-        for j, c in each():
+        for j, c in each(halo):
             for point, factor, right_side, index in targets:
                 put(U, point, c, j, w[j][c] + factor * STEP * rate[j][c] + at(right_side, index, c, j))
 
     def coarsest(k):
         w, rate = rates(Fx, k + 4)
-        for j, c in each():
+        for j, c in each(halo=k == 0):
             base = at(S, k, c, j) + 16 * STEP * at(R0, k, c, j)
             index = (k + 8) // 4
             g = coarse_rhs(at(G3, index, c, j), at(S, k + 8, c, j), w[j][c] + 8 * STEP * rate[j][c], base)
@@ -446,6 +448,7 @@
 
     fields_a = ((Fx, 4), (G3, 2))
     fields_b = ((Fx, 12), (G3, 3))
+    fine(0, True)
     halos_of(*arrivals[0])
     descend(0)
     halos_of(*arrivals[1])
@@ -456,15 +459,15 @@
     exchange(5, fields_b)
     exchanged(4, fields_a)
     coarsest(0)
-    ascend(6, ((7, 2, G1, 7),))
+    ascend(6, ((7, 2, G1, 7),), halo=False)
     return_points(1)
     descend(3)
     exchanged(5, fields_b)
     coarsest(8)
     ascend(8, ((9, 2, G1, 9), (10, 4, G2, 5), (12, 8, G3, 3), (16, 16, G4, 0)))
-    ascend(10, ((11, 2, G1, 11),))
+    ascend(10, ((11, 2, G1, 11),), halo=False)
     ascend(12, ((13, 2, G1, 13), (14, 4, G2, 7)))
-    ascend(14, ((15, 2, G1, 15),))
+    ascend(14, ((15, 2, G1, 15),), halo=False)
     return_points(9)
 
     def side_edge(t):

time: 85.3 us -> 84.8 us (level)
  no operation moved by 1% of the time
where the time goes in v7:
time: 84.8 us; the launch traced here: 84.2 us
  Pallas kernels  82.9 us (98%)
  local copies, waits for them, and re-layouts  1.32 us (2%)
    pallas_call x1, Pallas kernels, body(): pl.pallas_call(kernel, out_shape=pltpu.VMEM((2, 2, BLOCK_ROWS, BLOCK_COLS...  82.9 us

profile of v7, /device:TPU:2, one launch (start us, length us, event | category | flops | bytes accessed | tf_op | source)
XLA Modules:
  0.0 84.2 jit_solution(14830010515467485774)
XLA Ops:
  0.0 82.9 %cycle.1 = f32[2,2,256,512]{3,2,1,0:T(8,128)S(1)} custom-call(f32[2,256,512]{2,1,0:T(8,128)} %initial.1, f32[2,256,512]{2,1,0:T(8,128)} %forcing.1, f32[1,2,256,512]{3,2,1,0:T(8,128)} %guess.1), custom_call_target="tpu_custom_call" | custom-call | tf_op jit(solution)/shard_map/cycle/pallas_call | solution.py:664
  82.9 1.3 %copy.5 = f32[2,2,256,512]{3,2,1,0:T(8,128)} copy(f32[2,2,256,512]{3,2,1,0:T(8,128)S(1)} %cycle.1) | data formatting | bytes 4194304

commit v8 on v7

--- a/solution.py
+++ b/solution.py
@@ -353,13 +353,13 @@
         residual = g - (point - image)
         return residual + point - base
 
-    def fine(k, relaxes):
+    def fine(k, relaxes, halo=True):
         w, rate = rates(S, k)
         for j, c in each():
             put(R0, k, c, j, rate[j][c])
             put(T1, k, c, j, w[j][c] + STEP * rate[j][c])
         w, rate = rates(T1, k)
-        for j, c in each():
+        for j, c in each(halo):
             base = at(S, k, c, j) + 2 * STEP * at(R0, k, c, j)
             g = coarse_rhs(0.0, at(S, k + 1, c, j), w[j][c] + STEP * rate[j][c], base)
             put(G1, k + 1, c, j, g)
@@ -367,27 +367,22 @@
                 put(Fx, k + 1, c, j, base + g)
 
     def descend(q):
-        def fine_pair(i, carry):
-            fine(4 * q + 2 * i, True)
-            fine(4 * q + 2 * i + 1, False)
-            return carry
-
-        if q == 0:
-            fine(1, False)
-        lax.fori_loop(0 if q > 0 else 1, 2, fine_pair, 0)
-
-        def second(i, carry):
+        if q > 0:
+            fine(4 * q, True)
+        fine(4 * q + 1, False)
+        fine(4 * q + 2, True)
+        fine(4 * q + 3, False, halo=False)
+
+        for i in range(2):
             m = 2 * q + i
             k = 2 * m
             w, rate = rates(Fx, k + 1)
-            for j, c in each():
+            for j, c in each(halo=i == 0):
                 base = at(S, k, c, j) + 4 * STEP * at(R0, k, c, j)
                 g = coarse_rhs(at(G1, k + 2, c, j), at(S, k + 2, c, j), w[j][c] + 2 * STEP * rate[j][c], base)
                 put(G2, m + 1, c, j, g)
-                put(Fx, k + 2, c, j, base + g)
-            return carry
-
-        lax.fori_loop(0, 2, second, 0)
+                if i == 0:
+                    put(Fx, k + 2, c, j, base + g)
 
         k = 4 * q
         w, rate = rates(Fx, k + 2)

time: 84.8 us -> 84.3 us (level)
  no operation moved by 1% of the time
where the time goes in v8:
time: 84.3 us; the launch traced here: 83.7 us
  Pallas kernels  82.4 us (98%)
  local copies, waits for them, and re-layouts  1.32 us (2%)
    pallas_call x1, Pallas kernels, body(): pl.pallas_call(kernel, out_shape=pltpu.VMEM((2, 2, BLOCK_ROWS, BLOCK_COLS...  82.4 us

profile of v8, /device:TPU:2, one launch (start us, length us, event | category | flops | bytes accessed | tf_op | source)
XLA Modules:
  0.0 83.7 jit_solution(775104442013746106)
XLA Ops:
  0.0 82.4 %cycle.1 = f32[2,2,256,512]{3,2,1,0:T(8,128)S(1)} custom-call(f32[2,256,512]{2,1,0:T(8,128)} %initial.1, f32[2,256,512]{2,1,0:T(8,128)} %forcing.1, f32[1,2,256,512]{3,2,1,0:T(8,128)} %guess.1), custom_call_target="tpu_custom_call" | custom-call | tf_op jit(solution)/shard_map/cycle/pallas_call | solution.py:659
  82.4 1.3 %copy.5 = f32[2,2,256,512]{3,2,1,0:T(8,128)} copy(f32[2,2,256,512]{3,2,1,0:T(8,128)S(1)} %cycle.1) | data formatting | bytes 4194304
